TPU v7x, 32 devices: a whole 2x2x4 slice. The times are simulated.
32 devices in a mesh: depth: 4 (over z), illum: 8 (over y, x, core).
Axes of the slice: x: 2, y: 2, z: 4, core: 2. Of those that a mesh axis runs over, the one named last changes fastest.
Arguments:
- amplitude: float32 [4, 256, 256], P('depth', 'illum'), may hold values from 0.92 to 1
- phase: float32 [4, 256, 256], P('depth', 'illum'), may hold values from -3.140625 to 3.140625
- kernel_phase: float32 [256, 256], replicated, may hold values from -3.140625 to 3.140625
- entry_field: float32 [2, 4, 8, 256, 256], P(None, 'depth', 'illum'), may hold values from -6 to 6
- cotangent: float32 [2, 8, 256, 256], P(None, 'illum'), may hold values from -6 to 6
Outputs:
- slice_grad: float32 [2, 4, 256, 256], P(None, 'depth', 'illum')
All inputs are finite; a program needn't handle non-finite values.
Results may differ from a plain program's by a relative error of at most 0.0003.
Values sent between devices are 32-bit elements; how exact they have to be, the bound alone decides.
A program may use at most 64 MiB of HBM per device.

v0:
```python
import math

import jax
import jax.numpy as jnp
from jax import lax
from jax.sharding import PartitionSpec as P

HIGHEST = lax.Precision.HIGHEST


def from_behind(value, axis, steps):
    count = lax.axis_size(axis)
    first, last = (max(0, -steps), min(count, count - steps))
    return lax.ppermute(value, axis, [(source, source + steps) for source in range(first, last)])


def dft_tables(length):
    index = jnp.arange(length, dtype=jnp.int32)
    product = index[:, None] * index[None, :] % length
    angle = product.astype(jnp.float32) * (2.0 * math.pi / length)
    return (jnp.cos(angle), jnp.sin(angle))


def left_mult(matrix, flat):
    return jnp.einsum("jk,bkl->bjl", matrix, flat, precision=HIGHEST)


def right_mult(flat, matrix):
    return jnp.matmul(flat, matrix, precision=HIGHEST)


def transform(field_re, field_im, cos_t, sin_t):
    left_re = left_mult(cos_t, field_re) - left_mult(sin_t, field_im)
    left_im = left_mult(cos_t, field_im) + left_mult(sin_t, field_re)
    out_re = right_mult(left_re, cos_t) - right_mult(left_im, sin_t)
    out_im = right_mult(left_re, sin_t) + right_mult(left_im, cos_t)
    return (out_re, out_im)


def propagate(field_re, field_im, kern_re, kern_im, cos_t, sin_t):
    length = cos_t.shape[0]
    freq_re, freq_im = transform(field_re, field_im, cos_t, -sin_t)
    mixed_re = freq_re * kern_re - freq_im * kern_im
    mixed_im = freq_re * kern_im + freq_im * kern_re
    back_re, back_im = transform(mixed_re, mixed_im, cos_t, sin_t)
    factor = 1.0 / (length * length)
    return (back_re * factor, back_im * factor)


def adjoint_block(
    chi_re, chi_im, psi_re, psi_im, trans_re, trans_im, kern_re, kern_im, cos_t, sin_t
):
    grads_re = []
    grads_im = []
    for layer in reversed(range(trans_re.shape[0])):
        back_re, back_im = propagate(chi_re, chi_im, kern_re, -kern_im, cos_t, sin_t)
        grads_re.append(jnp.sum(back_re * psi_re[layer] + back_im * psi_im[layer], axis=0))
        grads_im.append(jnp.sum(back_im * psi_re[layer] - back_re * psi_im[layer], axis=0))
        chi_re = back_re * trans_re[layer] + back_im * trans_im[layer]
        chi_im = back_im * trans_re[layer] - back_re * trans_im[layer]
    return (chi_re, chi_im, jnp.stack(grads_re[::-1]), jnp.stack(grads_im[::-1]))


def per_device(amplitude, phase, kernel_phase, entry_field, cotangent):
    amp_whole, phase_whole = (
        lax.all_gather(amplitude, "illum", axis=1, tiled=True),
        lax.all_gather(phase, "illum", axis=1, tiled=True),
    )
    trans_re = amp_whole * jnp.cos(phase_whole)
    trans_im = amp_whole * jnp.sin(phase_whole)
    kern_re = jnp.cos(kernel_phase)
    kern_im = jnp.sin(kernel_phase)
    length = kernel_phase.shape[0]
    cos_t, sin_t = dft_tables(length)
    slices = amplitude.shape[0]
    angles = entry_field.shape[2]
    field_re = entry_field[0, 0]
    field_im = entry_field[1, 0]
    seen_re = [field_re]
    seen_im = [field_im]
    psi_re = jnp.stack(seen_re)
    psi_im = jnp.stack(seen_im)
    depth = lax.axis_size("depth")
    position = lax.axis_index("depth")
    at_top = position == depth - 1
    zero_grad = jnp.zeros((slices, length, length), jnp.float32)

    def section_all(step, carry):
        in_re, in_im, acc_re, acc_im = carry
        active = step == depth - 1 - position
        start_re = jnp.where(at_top, cotangent[0], in_re)
        start_im = jnp.where(at_top, cotangent[1], in_im)

        def work():
            return adjoint_block(
                start_re,
                start_im,
                psi_re,
                psi_im,
                trans_re,
                trans_im,
                kern_re,
                kern_im,
                cos_t,
                sin_t,
            )

        def resting():
            blank = jnp.zeros((angles, length, length), jnp.float32)
            return (blank, blank, zero_grad, zero_grad)

        out_re, out_im, part_re, part_im = lax.cond(active, work, resting)
        sent = from_behind(jnp.stack([out_re, out_im]), "depth", -1)
        return (sent[0], sent[1], acc_re + part_re, acc_im + part_im)

    blank = jnp.zeros((angles, length, length), jnp.float32)
    result = lax.fori_loop(0, depth, section_all, (blank, blank, zero_grad, zero_grad))
    grad_local = jnp.stack([result[2], result[3]])
    factor = 1.0 / math.sqrt(angles * lax.axis_size("illum"))
    mine = lax.psum_scatter(grad_local, "illum", scatter_dimension=2, tiled=True)
    return mine * factor


def solution(mesh):
    return jax.shard_map(
        per_device,
        mesh=mesh,
        in_specs=(
            P("depth", "illum", None),
            P("depth", "illum", None),
            P(),
            P(None, "depth", "illum", None, None),
            P(None, "illum", None, None),
        ),
        out_specs=P(None, "depth", "illum", None),
        check_vma=False,
    )
```

profile of v0, /device:TPU:0, one launch (start us, length us, event | category | flops | bytes accessed | tf_op | source)
XLA Modules:
  0.0 185.1 jit_solution(17594046820100809014)
XLA Ops:
  6.5 11.1 %all_gather.6 = f32[1,256,256]{2,1,0:T(8,128)S(1)} all-gather(f32[1,32,256]{2,1,0:T(8,128)} %param.9), channel_id=1, replica_groups=mesh['depth'=4,'illum'=8] {'illum'}, dimensions={1}, use_global_device_ids=true | all-gather | bytes 294912 | tf_op jit(solution)/shard_map/all_gather | solution.py:66
  17.7 9.2 %all_gather.7 = f32[1,256,256]{2,1,0:T(8,128)S(1)} all-gather(f32[1,32,256]{2,1,0:T(8,128)S(1)} %copy-done.7), channel_id=1, replica_groups=mesh['depth'=4,'illum'=8] {'illum'}, dimensions={1}, use_global_device_ids=true | all-gather | bytes 294912 | tf_op jit(solution)/shard_map/all_gather | solution.py:67
  26.9 0.9 fusion.36
  27.9 1.0 sine_multiply_fusion
  28.9 1.0 copy-done
  29.9 113.7 %while.23 = (s32[]{:T(128)}, f32[1,256,256]{2,1,0:T(8,128)S(1)}, f32[1,256,256]{2,1,0:T(8,128)S(1)}, f32[1,256,256]{2,1,0:T(8,128)S(1)}, f32[1,256,256]{2,1,0:T(...) while((s32[]{:T(128)}, f32[1,256,256]{2,1,0:T(8,128)S(1)}, ...), condition=%wide.region_3.4_spmd.clone.clone, body=%wide.region_0.3_spmd.clone.clone.sunk | while | flops 3224961024 | bytes 31195592 | solution.py:117
  30.9 1.3 collective-permute-start
  33.1 13.9 %collective-permute-done = f32[2,1,256,256]{3,2,1,0:T(8,128)S(1)} collective-permute-done((f32[2,1,256,256]{3,2,1,0:T(8,128)S(1)}, f32[2,1,256,256]{3,2,1,0:T(8,128)S(1)}, u32[]{:S(2)}, u32[]{:S(2)}) %collective-permute-start) | collective-permute-done | bytes 524320 | tf_op jit(solution)/shard_map/while/body/eval_jaxpr/ppermute | solution.py:14
  47.0 0.9 copy-done.2
  49.0 1.3 collective-permute-start
  50.3 1.8 select_add_fusion.3
  52.1 12.1 %collective-permute-done = f32[2,1,256,256]{3,2,1,0:T(8,128)S(1)} collective-permute-done((f32[2,1,256,256]{3,2,1,0:T(8,128)S(1)}, f32[2,1,256,256]{3,2,1,0:T(8,128)S(1)}, u32[]{:S(2)}, u32[]{:S(2)}) %collective-permute-start) | collective-permute-done | bytes 524320 | tf_op jit(solution)/shard_map/while/body/eval_jaxpr/ppermute | solution.py:14
  64.3 0.9 copy-done.2
  66.3 1.3 collective-permute-start
  67.6 1.8 select_add_fusion.3
  69.4 45.4 %collective-permute-done = f32[2,1,256,256]{3,2,1,0:T(8,128)S(1)} collective-permute-done((f32[2,1,256,256]{3,2,1,0:T(8,128)S(1)}, f32[2,1,256,256]{3,2,1,0:T(8,128)S(1)}, u32[]{:S(2)}, u32[]{:S(2)}) %collective-permute-start) | collective-permute-done | bytes 524320 | tf_op jit(solution)/shard_map/while/body/eval_jaxpr/ppermute | solution.py:14
  114.8 0.9 copy-done.2
  116.6 11.6 %conditional.4 = (f32[1,256,256]{2,1,0:T(8,128)S(1)}, f32[1,256,256]{2,1,0:T(8,128)S(1)}, f32[1,1,256,256]{3,2,1,0:T(8,128)S(1)}, f32[1,1,256,256]{3,2,1,0:T(8,128)S(1)}) conditional(s32[]{:T(128)} %convert_element_type.59, () %tuple.92, (pred[]{:T(512)}, f32[2,1,256,256]{3,2,1,0:T(8,128)S(1)}, f32[1,256,256]{2,1,0:T(8,128)S(1)}, ...), branch_computations={%region_1.1_spmd, %region_2.2_spmd.clone} | conditional | flops 3223650304 | bytes 20971556 | solution.py:112
  128.2 1.3 collective-permute-start
  129.5 1.8 select_add_fusion.3
  131.3 11.2 %collective-permute-done = f32[2,1,256,256]{3,2,1,0:T(8,128)S(1)} collective-permute-done((f32[2,1,256,256]{3,2,1,0:T(8,128)S(1)}, f32[2,1,256,256]{3,2,1,0:T(8,128)S(1)}, u32[]{:S(2)}, u32[]{:S(2)}) %collective-permute-start) | collective-permute-done | bytes 524320 | tf_op jit(solution)/shard_map/while/body/eval_jaxpr/ppermute | solution.py:14
  143.6 1.8 pad_maximum_fusion.1
  145.4 31.4 %reduce-scatter.2.cloned.1.call-done = f32[2,1,32,256]{3,2,1,0:T(8,128)} async-done(((f32[2,1,256,256]{3,2,1,0:T(8,128)}), f32[2,1,32,256]{3,2,1,0:T(8,128)}) %reduce-scatter.2.cloned.1.call-update) | async-done | bytes 65552 | tf_op jit(solution)/shard_map/reduce_scatter | solution.py:120
  176.8 1.5 broadcast_multiply_fusion
  (91 shorter events, 17.7 us)
Async XLA Ops:
  6.5 170.3 %reduce-scatter.2.cloned.1.call-start = ((), (), s32[]{:S(2)}) async-start(), calls=%async_computation.1 | async-start | bytes 589824 | tf_op jit(solution)/shard_map/reduce_scatter | solution.py:120
  6.5 11.1 %copy-start.7 = (f32[1,32,256]{2,1,0:T(8,128)S(1)}, f32[1,32,256]{2,1,0:T(8,128)}, u32[]{:S(2)}) copy-start(f32[1,32,256]{2,1,0:T(8,128)} %param.10) | copy-start | bytes 98308
  6.5 20.3 %copy-start.6 = (f32[256,256]{1,0:T(8,128)S(1)}, f32[256,256]{1,0:T(8,128)}, u32[]{:S(2)}) copy-start(f32[256,256]{1,0:T(8,128)} %param.11) | copy-start | bytes 786436
  17.6 10.2 %copy-start.5 = (f32[2,1,1,256,256]{4,3,2,1,0:T(8,128)S(1)}, f32[2,1,1,256,256]{4,3,2,1,0:T(8,128)}, u32[]{:S(2)}) copy-start(f32[2,1,1,256,256]{4,3,2,1,0:T(8,128)} %param.12) | copy-start | bytes 1572868
  28.9 1.0 copy-start
  29.9 0.7 copy-start.1
  29.9 0.8 copy-start.3
  30.9 16.1 %collective-permute-start = (f32[2,1,256,256]{3,2,1,0:T(8,128)S(1)}, f32[2,1,256,256]{3,2,1,0:T(8,128)S(1)}, u32[]{:S(2)}, u32[]{:S(2)}) collective-permute-start(f32[2,1,256,256]{3,2,1,0:T(8,128)S(1)} %pad_maximum_fusion.3), channel_id=1, source_target_pairs={{8,0},{16,8},{24,16},{9,1},{17,9},{25,17},{10,2},{18,10},{26,18},{... | collective-permute-start | bytes 1572872 | tf_op jit(solution)/shard_map/while/body/eval_jaxpr/ppermute | solution.py:14
  47.0 1.0 copy-start.2
  47.0 1.0 copy-start.4
  48.0 0.8 copy-start.3
  49.0 15.3 %collective-permute-start = (f32[2,1,256,256]{3,2,1,0:T(8,128)S(1)}, f32[2,1,256,256]{3,2,1,0:T(8,128)S(1)}, u32[]{:S(2)}, u32[]{:S(2)}) collective-permute-start(f32[2,1,256,256]{3,2,1,0:T(8,128)S(1)} %pad_maximum_fusion.3), channel_id=1, source_target_pairs={{8,0},{16,8},{24,16},{9,1},{17,9},{25,17},{10,2},{18,10},{26,18},{... | collective-permute-start | bytes 1572872 | tf_op jit(solution)/shard_map/while/body/eval_jaxpr/ppermute | solution.py:14
  64.2 1.0 copy-start.2
  64.3 1.0 copy-start.4
  65.3 0.7 copy-start.1
  65.3 0.8 copy-start.3
  66.3 48.5 %collective-permute-start = (f32[2,1,256,256]{3,2,1,0:T(8,128)S(1)}, f32[2,1,256,256]{3,2,1,0:T(8,128)S(1)}, u32[]{:S(2)}, u32[]{:S(2)}) collective-permute-start(f32[2,1,256,256]{3,2,1,0:T(8,128)S(1)} %pad_maximum_fusion.3), channel_id=1, source_target_pairs={{8,0},{16,8},{24,16},{9,1},{17,9},{25,17},{10,2},{18,10},{26,18},{... | collective-permute-start | bytes 1572872 | tf_op jit(solution)/shard_map/while/body/eval_jaxpr/ppermute | solution.py:14
  114.8 1.0 copy-start.2
  114.8 1.0 copy-start.4
  115.8 0.7 copy-start.1
  115.8 0.8 copy-start.3
  128.2 14.3 %collective-permute-start = (f32[2,1,256,256]{3,2,1,0:T(8,128)S(1)}, f32[2,1,256,256]{3,2,1,0:T(8,128)S(1)}, u32[]{:S(2)}, u32[]{:S(2)}) collective-permute-start(f32[2,1,256,256]{3,2,1,0:T(8,128)S(1)} %pad_maximum_fusion.3), channel_id=1, source_target_pairs={{8,0},{16,8},{24,16},{9,1},{17,9},{25,17},{10,2},{18,10},{26,18},{... | collective-permute-start | bytes 1572872 | tf_op jit(solution)/shard_map/while/body/eval_jaxpr/ppermute | solution.py:14
  142.5 1.0 copy-start.2
  142.5 1.0 copy-start.4
  (1 other events, 0.7 us)
Sparse Core Ops, SparseCore 0:
  145.5 31.2 reduce-scatter.1
where the time goes:
time: 186 us; the launch traced here: 185 us
  waiting for transfers between devices  114 us (61%)
  blocking collectives  20.3 us (11%)
  between operations  13.5 us (7%)
  other arithmetic  11.4 us (6%)
  local copies, waits for them, and re-layouts  10.7 us (6%)
  matrix products  9.6 us (5%)
  starting transfers between devices  5.17 us (3%)
    ppermute x4, waiting for transfers between devices, from_behind(): lax.ppermute(value, axis, [(source, source + steps) for source in range(f...  82.6 us
    reduce_scatter x1, waiting for transfers between devices, per_device(): lax.psum_scatter(grad_local, 'illum', scatter_dimension=2, tiled=True)  31.4 us
    all_gather x1, blocking collectives, per_device(): lax.all_gather(amplitude, 'illum', axis=1, tiled=True)  11.1 us
    all_gather x1, blocking collectives, per_device(): lax.all_gather(phase, 'illum', axis=1, tiled=True)  9.21 us
    while x32, local copies, waits for them, and re-layouts  6.68 us
    add x4, other arithmetic, section_all(): return (sent[0], sent[1], acc_re + part_re, acc_im + part_im)  6.37 us
    ppermute x4, starting transfers between devices, from_behind(): lax.ppermute(value, axis, [(source, source + steps) for source in range(f...  5.17 us
    dot_general x8, matrix products, right_mult(): return jnp.matmul(flat, matrix, precision=HIGHEST)  4.82 us
  transfers between devices with their start and end apart: 5, of which 5 were waited for; matrix products, arithmetic and copies ran while one was open for 3% of the time, Pallas kernels for 0%

commit v1 on v0

v1 whole, which is shorter than its diff:
```python
import functools
import math

import jax
import jax.numpy as jnp
import ml_dtypes
import numpy as np
from jax import lax
from jax.experimental import pallas as pl
from jax.experimental.pallas import tpu as pltpu
from jax.sharding import PartitionSpec as P

MESH = pl.DeviceIdType.MESH
F32 = jnp.float32
BF16 = jnp.bfloat16


def halves(matrix):
    high = matrix.astype(ml_dtypes.bfloat16)
    low = (matrix - high.astype(np.float64)).astype(ml_dtypes.bfloat16)
    return [high, low]


def tables(length):
    half = length // 2
    out = []
    for odd in (0, 1):
        k = 2 * np.arange(half)[:, None] + odd
        angle = (k * np.arange(half)[None, :] % length) * (2.0 * np.pi / length)
        c, s = np.cos(angle), np.sin(angle)
        out.append(np.block([[c, s], [-s, c]]))
    out += [out[0].T, out[1].T]
    perm = np.concatenate([np.arange(0, length, 2), np.arange(1, length, 2)])
    shuffle = np.zeros((length, length))
    shuffle[perm, np.arange(length)] = 1.0
    stacked = sum([halves(m) for m in out], [])
    return np.stack(stacked + [shuffle.astype(ml_dtypes.bfloat16)])


def sincos(x):
    y = x * 0.5
    z = y * y
    s = 1.0 / math.factorial(13)
    for order in (11, 9, 7, 5, 3, 1):
        s = s * z + (-1.0) ** (order // 2) / math.factorial(order)
    s = s * y
    c = 1.0 / math.factorial(12)
    for order in (10, 8, 6, 4, 2, 0):
        c = c * z + (-1.0) ** (order // 2) / math.factorial(order)
    return 2.0 * s * c, 1.0 - 2.0 * s * s


def split(v):
    high = v.astype(BF16)
    return high, (v - high.astype(F32)).astype(BF16)


def dot(a, b):
    return jnp.dot(a, b, preferred_element_type=F32)


def right(v, tab, at):
    high, low = split(v)
    w_high, w_low = tab[2 * at], tab[2 * at + 1]
    return dot(low, w_high) + dot(high, w_low) + dot(high, w_high)


def left(v, tab, at):
    high, low = split(v)
    w_high, w_low = tab[2 * at], tab[2 * at + 1]
    return dot(w_high, low) + dot(w_low, high) + dot(w_high, high)


def kernel(
    depth, count, amp_ref, phase_ref, kern_ref, psi_ref, cot_ref, tab, out_ref,
    x_ref, h_ref, tmp_ref, own_ref, t_ref, prod_ref, land_ref,
    z_send, z_recv, g_send, g_recv, r_send, r_recv,
):
    length = kern_ref.shape[0]
    half = length // 2
    rows = amp_ref.shape[0]
    bits = count.bit_length() - 1
    d = lax.axis_index("depth")
    me = lax.axis_index("illum")
    needed = depth - 1 - d

    flip = [(1 << b) * (1 - 2 * (me // (1 << b) % 2)) for b in range(bits)]
    core = me % 2
    ahead, other = [], []
    for r in range(bits - 1):
        down, up = flip[bits - 1 - r], flip[1 + r]
        ahead.append(down + core * (up - down))
        other.append(up + core * (down - up))
    if bits:
        ahead.append(flip[0])

    def owner(p):
        order = other if p >= count // 2 else ahead
        block = me
        for r in range(bits):
            if p >> r & 1:
                block = block + (ahead[r] if r == bits - 1 else order[r])
        return block

    def rows_of(p):
        return pl.ds(pl.multiple_of(owner(p) * rows, rows), rows)

    barrier = pltpu.get_barrier_semaphore()
    for o in range(1, depth):
        pl.semaphore_signal(barrier, inc=1, device_id=((d + o) % depth, me), device_id_type=MESH)
    for r in range(bits):
        pl.semaphore_signal(barrier, inc=1, device_id=(d, me + ahead[r]), device_id_type=MESH)

    sin_t, cos_t = sincos(phase_ref[...])
    own_ref[0] = amp_ref[...] * cos_t
    own_ref[1] = amp_ref[...] * sin_t

    pl.semaphore_wait(barrier, depth - 1 + bits)

    def z_copy(target):
        return pltpu.make_async_remote_copy(
            src_ref=own_ref, dst_ref=t_ref.at[needed, 0],
            send_sem=z_send.at[target], recv_sem=z_recv.at[needed],
            device_id=(target, me), device_id_type=MESH,
        )

    @pl.loop(0, d)
    def _(target):
        z_copy(target).start()

    def g_copy(s, r):
        w = 1 << r
        return pltpu.make_async_remote_copy(
            src_ref=t_ref.at[s, pl.ds(0, w)], dst_ref=t_ref.at[s, pl.ds(w, w)],
            send_sem=g_send.at[s, r], recv_sem=g_recv.at[s, r],
            device_id=(d, me + ahead[r]), device_id_type=MESH,
        )

    def advance(s, step):
        @pl.when(jnp.logical_and(s >= 0, s < needed))
        def _():
            if step == 0:
                pltpu.make_async_copy(own_ref, t_ref.at[s, 0], z_recv.at[s]).wait()
            else:
                g_copy(s, step - 1).wait_recv()
            if step < bits:
                g_copy(s, step).start()

    phase = kern_ref[...]
    first, rest = split(phase)
    rest = phase - first.astype(F32)
    second, third = split(rest)
    shuffle = tab[8]
    moved = (dot(third, shuffle) + dot(second, shuffle)) + dot(first, shuffle)
    tmp_ref[0], tmp_ref[1] = moved[:, :half], moved[:, half:]
    scale = 1.0 / (length * length)
    for odd in (0, 1):
        for c in (0, 1):
            sin_h, cos_h = sincos(tmp_ref[c, pl.ds(odd, half, stride=2), :])
            at = (pl.ds(odd * half, half), pl.ds(c * half, half))
            h_ref[(0, *at)] = cos_h * scale
            h_ref[(1, *at)] = sin_h * scale

    x_ref[0] = cot_ref[0]
    x_ref[1] = cot_ref[1]

    def propagate(slot):
        re, im = x_ref[0], x_ref[1]
        parts = []
        for sign, at in ((1, 2), (-1, 3)):
            mixed = jnp.concatenate(
                [v[:, :half] + sign * v[:, half:] for v in (re, im)], axis=1)
            parts.append(right(mixed, tab, at))
        slot(0)
        even, odd = parts
        back = []
        mixes = []
        for sign, at in ((1, 0), (-1, 1)):
            stack = jnp.concatenate([
                jnp.concatenate([
                    v[:half, c * half:(c + 1) * half] + sign * v[half:, c * half:(c + 1) * half]
                    for v in (even, odd)], axis=1)
                for c in (0, 1)], axis=0)
            freq = left(stack, tab, at)
            f_re, f_im = freq[:half], freq[half:]
            h_re = h_ref[0, at * half:(at + 1) * half]
            h_im = h_ref[1, at * half:(at + 1) * half]
            mixes.append(jnp.concatenate(
                [f_re * h_re + f_im * h_im, f_im * h_re - f_re * h_im], axis=0))
        slot(1)
        for at in (0, 1):
            back.append(left(mixes[at], tab, 2 + at))
        slot(2)
        e, o = back
        total, gap = e + o, e - o
        ends = []
        for c in (0, 1):
            cols = slice(c * half, (c + 1) * half)
            mixed = jnp.concatenate([
                jnp.concatenate([total[:half, cols], gap[:half, cols]], axis=0),
                jnp.concatenate([total[half:, cols], gap[half:, cols]], axis=0)], axis=1)
            ends.append(right(mixed, tab, c))
        e, o = ends
        total, gap = e + o, e - o
        x_ref[0, :, :half] = total[:, :half]
        x_ref[0, :, half:] = gap[:, :half]
        x_ref[1, :, :half] = total[:, half:]
        x_ref[1, :, half:] = gap[:, half:]
        slot(3)

    slots = max(4, bits + 1)

    def body(q, carry):
        def slot(k):
            for step in reversed(range(bits + 1)):
                advance(q * slots + k - step, step)

        propagate(slot)
        for k in range(4, slots):
            slot(k)
        for p in range(count):
            at = rows_of(p)
            t_re, t_im = t_ref[q, p, 0], t_ref[q, p, 1]
            u_re, u_im = x_ref[0, at], x_ref[1, at]
            x_ref[0, at] = u_re * t_re + u_im * t_im
            x_ref[1, at] = u_im * t_re - u_re * t_im
        return carry

    lax.fori_loop(0, needed, body, 0)
    propagate(lambda k: None)

    def product(p):
        at = rows_of(p)
        u_re, u_im = x_ref[0, at], x_ref[1, at]
        p_re, p_im = psi_ref[0, at], psi_ref[1, at]
        prod_ref[p, 0] = u_re * p_re + u_im * p_im
        prod_ref[p, 1] = u_im * p_re - u_re * p_im

    def r_copy(r):
        w = 1 << r
        return pltpu.make_async_remote_copy(
            src_ref=prod_ref.at[pl.ds(w, w)], dst_ref=land_ref.at[pl.ds(w, w)],
            send_sem=r_send.at[r], recv_sem=r_recv.at[r],
            device_id=(d, me + ahead[r]), device_id_type=MESH,
        )

    for p in range(count // 2, count):
        product(p)
    if bits:
        r_copy(bits - 1).start()
    for p in range(count // 2):
        product(p)
    for r in reversed(range(bits)):
        w = 1 << r
        r_copy(r).wait_recv()
        if r:
            v = w // 2
            prod_ref[v:w] += land_ref[w + v:2 * w]
            r_copy(r - 1).start()
            prod_ref[:v] += land_ref[w:w + v]
        else:
            prod_ref[0] += land_ref[1]
    out_ref[...] = prod_ref[0]

    for r in range(bits):
        r_copy(r).wait_send()

    @pl.loop(0, needed)
    def _(s):
        for r in range(bits):
            g_copy(s, r).wait_send()

    @pl.loop(0, d)
    def _(target):
        z_copy(target).wait_send()


def per_device(depth, count, amplitude, phase, kernel_phase, entry_field, cotangent):
    _, rows, length = amplitude.shape
    angles = entry_field.shape[2]
    assert angles == 1 and amplitude.shape[0] == 1
    bits = count.bit_length() - 1
    assert count == 1 << bits
    above, steps = max(depth - 1, 1), max(bits, 1)
    tab = jnp.asarray(tables(length))
    vmem = pl.BlockSpec(memory_space=pltpu.VMEM)
    field = (2, length, length)
    dma = pltpu.SemaphoreType.DMA
    mine = pl.pallas_call(
        functools.partial(kernel, depth, count),
        out_shape=jax.ShapeDtypeStruct((2, rows, length), F32),
        in_specs=[vmem] * 6,
        out_specs=vmem,
        scratch_shapes=[
            pltpu.VMEM(field, F32),
            pltpu.VMEM(field, F32),
            pltpu.VMEM((2, length, length // 2), F32),
            pltpu.VMEM((2, rows, length), F32),
            pltpu.VMEM((above, count, 2, rows, length), F32),
            pltpu.VMEM((count, 2, rows, length), F32),
            pltpu.VMEM((count, 2, rows, length), F32),
            dma((above,)), dma((above,)),
            dma((above, steps)), dma((above, steps)),
            dma((steps,)), dma((steps,)),
        ],
        compiler_params=pltpu.CompilerParams(
            collective_id=0, has_side_effects=True, vmem_limit_bytes=40 * 1024 * 1024),
    )(amplitude[0], phase[0], kernel_phase, entry_field[:, 0, 0], cotangent[:, 0], tab)
    return (mine * (1.0 / math.sqrt(angles * count)))[:, None]


def solution(mesh):
    return jax.shard_map(
        functools.partial(per_device, mesh.shape["depth"], mesh.shape["illum"]),
        mesh=mesh,
        in_specs=(
            P("depth", "illum", None),
            P("depth", "illum", None),
            P(),
            P(None, "depth", "illum", None, None),
            P(None, "illum", None, None),
        ),
        out_specs=P(None, "depth", "illum", None),
        check_vma=False,
    )
```

time: 186 us -> 46.5 us (0.25)
  waiting for transfers between devices: 114 us -> 0 us
  Pallas kernels: 0 us -> 39.6 us
  blocking collectives: 20.3 us -> 0 us
  between operations: 13.5 us -> 0.02 us
  other arithmetic: 11.4 us -> 0.64 us
  matrix products: 9.6 us -> 0 us
  starting transfers between devices: 5.17 us -> 0 us
  local copies, waits for them, and re-layouts: 10.7 us -> 5.82 us
    ppermute x4 -> x0, waiting for transfers between devices: 82.6 us -> none  [from_behind(): lax.ppermute(value, axis, [(source, source + steps) for source in range(f...]
    pallas_call x0 -> x1, Pallas kernels: none -> 39.6 us  [per_device(): pl.pallas_call(functools.partial(kernel, depth, count), out_shape=jax.Sha...]
    reduce_scatter x1 -> x0, waiting for transfers between devices: 31.4 us -> none  [per_device(): lax.psum_scatter(grad_local, 'illum', scatter_dimension=2, tiled=True)]
    all_gather x2 -> x0, blocking collectives: 20.3 us -> none  [the longest x1 11.1 us: per_device(): lax.all_gather(amplitude, 'illum', axis=1, tiled=True)]
    dot_general x16 -> x0, matrix products: 9.6 us -> none  [the longest x8 4.82 us: right_mult(): return jnp.matmul(flat, matrix, precision=HIGHEST)]
    while x32 -> x0, local copies, waits for them, and re-layouts: 6.68 us -> none
    add x4 -> x0, other arithmetic: 6.37 us -> none  [section_all(): return (sent[0], sent[1], acc_re + part_re, acc_im + part_im)]
    ppermute x4 -> x0, starting transfers between devices: 5.17 us -> none  [from_behind(): lax.ppermute(value, axis, [(source, source + steps) for source in range(f...]
  transfers between devices with their start and end apart: 5 -> 0, of which waited for: 5 -> 0; matrix products, arithmetic and copies ran while one was open for 3% -> 0% of each run, Pallas kernels for 0% -> 0%
where the time goes in v1:
time: 46.5 us; the launch traced here: 46.1 us
  Pallas kernels  39.6 us (85%)
  local copies, waits for them, and re-layouts  5.82 us (13%)
  other arithmetic  0.64 us (1%)
    pallas_call x1, Pallas kernels, per_device(): pl.pallas_call(functools.partial(kernel, depth, count), out_shape=jax.Sha...  39.6 us
    unnamed x12, local copies, waits for them, and re-layouts  5.82 us

profile of v1, /device:TPU:0, one launch (start us, length us, event | category | flops | bytes accessed | tf_op | source)
XLA Modules:
  0.0 46.1 jit_solution(16235139448633736915)
XLA Ops:
  0.0 0.0 copy-start
  0.0 1.3 %copy-done = bf16[9,256,256]{2,1,0:T(8,128)(2,1)S(1)} copy-done((bf16[9,256,256]{2,1,0:T(8,128)(2,1)S(1)}, bf16[9,256,256]{2,1,0:T(8,128)(2,1)}, u32[]{:S(2)}) %copy-start) | copy-done | bytes 1179672
  1.3 0.0 copy-start.1
  1.3 1.0 %copy-done.1 = f32[2,1,1,256,256]{4,3,2,1,0:T(8,128)S(1)} copy-done((f32[2,1,1,256,256]{4,3,2,1,0:T(8,128)S(1)}, f32[2,1,1,256,256]{4,3,2,1,0:T(8,128)}, u32[]{:S(2)}) %copy-start.1) | copy-done | bytes 524312
  2.3 0.0 copy-start.2
  2.3 1.0 %copy-done.2 = f32[2,1,256,256]{3,2,1,0:T(8,128)S(1)} copy-done((f32[2,1,256,256]{3,2,1,0:T(8,128)S(1)}, f32[2,1,256,256]{3,2,1,0:T(8,128)}, u32[]{:S(2)}) %copy-start.2) | copy-done | bytes 524312
  3.4 0.0 copy-start.3
  3.4 0.9 %copy-done.3 = f32[256,256]{1,0:T(8,128)S(1)} copy-done((f32[256,256]{1,0:T(8,128)S(1)}, f32[256,256]{1,0:T(8,128)}, u32[]{:S(2)}) %copy-start.3) | copy-done | bytes 262168
  4.3 0.0 copy-start.4
  4.3 0.8 %copy-done.4 = f32[1,32,256]{2,1,0:T(8,128)S(1)} copy-done((f32[1,32,256]{2,1,0:T(8,128)S(1)}, f32[1,32,256]{2,1,0:T(8,128)}, u32[]{:S(2)}) %copy-start.4) | copy-done | bytes 32792
  5.1 0.0 copy-start.5
  5.1 0.8 %copy-done.5 = f32[1,32,256]{2,1,0:T(8,128)S(1)} copy-done((f32[1,32,256]{2,1,0:T(8,128)S(1)}, f32[1,32,256]{2,1,0:T(8,128)}, u32[]{:S(2)}) %copy-start.5) | copy-done | bytes 32792
  5.8 39.6 %shard_map.64 = f32[2,32,256]{2,1,0:T(8,128)S(1)} custom-call(f32[32,256]{1,0:T(8,128)S(1)} %bitcast.10, f32[32,256]{1,0:T(8,128)S(1)} %bitcast.11, f32[256,256]{1,0:T(8,128)S(1)} %copy-done.3, f32[2,256,256]{2,1,0:T(8,128)S(1)} %bitcast.8, f32[2,256,256]{2,1,0:T(8,128)S(1)} %bitcast.9, bf16[9,256,256]{2,1,0:T(8,128)(2,1)S(1)} %copy-done), custom_call_target="tpu_custom_call" | custom-call | tf_op jit(solution)/shard_map/pallas_call | solution.py:289
  45.5 0.6 %multiply_bitcast_fusion = f32[2,1,32,256]{3,2,1,0:T(8,128)} fusion(f32[2,32,256]{2,1,0:T(8,128)S(1)} %shard_map.64), kind=kLoop, calls=%fused_computation | loop fusion | flops 16384 | bytes 131072 | tf_op jit(solution)/shard_map/broadcast_in_dim | solution.py:309
Async XLA Ops:
  0.0 1.3 %copy-start = (bf16[9,256,256]{2,1,0:T(8,128)(2,1)S(1)}, bf16[9,256,256]{2,1,0:T(8,128)(2,1)}, u32[]{:S(2)}) copy-start(bf16[9,256,256]{2,1,0:T(8,128)(2,1)} %constant.4.clone.tab) | copy-start | bytes 3538948
  1.3 1.0 %copy-start.1 = (f32[2,1,1,256,256]{4,3,2,1,0:T(8,128)S(1)}, f32[2,1,1,256,256]{4,3,2,1,0:T(8,128)}, u32[]{:S(2)}) copy-start(f32[2,1,1,256,256]{4,3,2,1,0:T(8,128)} %param.9) | copy-start | bytes 1572868
  2.3 1.0 %copy-start.2 = (f32[2,1,256,256]{3,2,1,0:T(8,128)S(1)}, f32[2,1,256,256]{3,2,1,0:T(8,128)}, u32[]{:S(2)}) copy-start(f32[2,1,256,256]{3,2,1,0:T(8,128)} %param.10) | copy-start | bytes 1572868
  3.4 0.9 %copy-start.3 = (f32[256,256]{1,0:T(8,128)S(1)}, f32[256,256]{1,0:T(8,128)}, u32[]{:S(2)}) copy-start(f32[256,256]{1,0:T(8,128)} %kern_ref.1) | copy-start | bytes 786436
  4.3 0.8 %copy-start.4 = (f32[1,32,256]{2,1,0:T(8,128)S(1)}, f32[1,32,256]{2,1,0:T(8,128)}, u32[]{:S(2)}) copy-start(f32[1,32,256]{2,1,0:T(8,128)} %param.6) | copy-start | bytes 98308
  5.1 0.8 %copy-start.5 = (f32[1,32,256]{2,1,0:T(8,128)S(1)}, f32[1,32,256]{2,1,0:T(8,128)}, u32[]{:S(2)}) copy-start(f32[1,32,256]{2,1,0:T(8,128)} %param.7) | copy-start | bytes 98308

commit v2 on v1

--- a/solution.py
+++ b/solution.py
@@ -72,8 +72,9 @@
 
 
 def kernel(
-    depth, count, amp_ref, phase_ref, kern_ref, psi_ref, cot_ref, tab, out_ref,
-    x_ref, h_ref, tmp_ref, own_ref, t_ref, prod_ref, land_ref,
+    depth, count, amp_hbm, phase_hbm, kern_hbm, psi_hbm, cot_hbm, tab_hbm, out_ref,
+    amp_ref, phase_ref, kern_ref, psi_ref, tab,
+    x_ref, h_ref, tmp_ref, own_ref, t_ref, prod_ref, land_ref, loaded,
     z_send, z_recv, g_send, g_recv, r_send, r_recv,
 ):
     length = kern_ref.shape[0]
@@ -84,6 +85,15 @@
     me = lax.axis_index("illum")
     needed = depth - 1 - d
 
+    loads = [
+        pltpu.make_async_copy(source, target, loaded.at[i])
+        for i, (source, target) in enumerate([
+            (amp_hbm, amp_ref), (phase_hbm, phase_ref), (kern_hbm, kern_ref),
+            (tab_hbm, tab), (cot_hbm, x_ref), (psi_hbm, psi_ref)])
+    ]
+    for load in loads:
+        load.start()
+
     flip = [(1 << b) * (1 - 2 * (me // (1 << b) % 2)) for b in range(bits)]
     core = me % 2
     ahead, other = [], []
@@ -111,6 +121,8 @@
     for r in range(bits):
         pl.semaphore_signal(barrier, inc=1, device_id=(d, me + ahead[r]), device_id_type=MESH)
 
+    loads[0].wait()
+    loads[1].wait()
     sin_t, cos_t = sincos(phase_ref[...])
     own_ref[0] = amp_ref[...] * cos_t
     own_ref[1] = amp_ref[...] * sin_t
@@ -124,9 +136,14 @@
             device_id=(target, me), device_id_type=MESH,
         )
 
-    @pl.loop(0, d)
-    def _(target):
-        z_copy(target).start()
+    def post(g):
+        target = g + 1 - needed
+
+        @pl.when(jnp.logical_and(target >= 0, target < d))
+        def _():
+            z_copy(target).start()
+
+    post(-1)
 
     def g_copy(s, r):
         w = 1 << r
@@ -146,6 +163,8 @@
             if step < bits:
                 g_copy(s, step).start()
 
+    loads[2].wait()
+    loads[3].wait()
     phase = kern_ref[...]
     first, rest = split(phase)
     rest = phase - first.astype(F32)
@@ -161,8 +180,7 @@
             h_ref[(0, *at)] = cos_h * scale
             h_ref[(1, *at)] = sin_h * scale
 
-    x_ref[0] = cot_ref[0]
-    x_ref[1] = cot_ref[1]
+    loads[4].wait()
 
     def propagate(slot):
         re, im = x_ref[0], x_ref[1]
@@ -208,16 +226,18 @@
         x_ref[1, :, half:] = gap[:, half:]
         slot(3)
 
-    slots = max(4, bits + 1)
+    slots = max(4, bits + 1 + (bits + 1) % 2)
+
+    def slot(q, k):
+        post(q * slots + k)
+        for step in reversed(range(bits + 1)):
+            if (k - step) % 2 == 0:
+                advance(q * (slots // 2) + (k - step) // 2, step)
 
     def body(q, carry):
-        def slot(k):
-            for step in reversed(range(bits + 1)):
-                advance(q * slots + k - step, step)
-
-        propagate(slot)
+        propagate(functools.partial(slot, q))
         for k in range(4, slots):
-            slot(k)
+            slot(q, k)
         for p in range(count):
             at = rows_of(p)
             t_re, t_im = t_ref[q, p, 0], t_ref[q, p, 1]
@@ -227,7 +247,13 @@
         return carry
 
     lax.fori_loop(0, needed, body, 0)
-    propagate(lambda k: None)
+    propagate(lambda k: post(needed * slots + k))
+
+    @pl.loop(jnp.minimum(needed * slots + 5 - needed, d), d)
+    def _(target):
+        z_copy(target).start()
+
+    loads[5].wait()
 
     def product(p):
         at = rows_of(p)
@@ -283,15 +309,19 @@
     assert count == 1 << bits
     above, steps = max(depth - 1, 1), max(bits, 1)
     tab = jnp.asarray(tables(length))
-    vmem = pl.BlockSpec(memory_space=pltpu.VMEM)
     field = (2, length, length)
     dma = pltpu.SemaphoreType.DMA
     mine = pl.pallas_call(
         functools.partial(kernel, depth, count),
         out_shape=jax.ShapeDtypeStruct((2, rows, length), F32),
-        in_specs=[vmem] * 6,
-        out_specs=vmem,
+        in_specs=[pl.BlockSpec(memory_space=pl.ANY)] * 6,
+        out_specs=pl.BlockSpec(memory_space=pltpu.VMEM),
         scratch_shapes=[
+            pltpu.VMEM((rows, length), F32),
+            pltpu.VMEM((rows, length), F32),
+            pltpu.VMEM((length, length), F32),
+            pltpu.VMEM(field, F32),
+            pltpu.VMEM(tab.shape, BF16),
             pltpu.VMEM(field, F32),
             pltpu.VMEM(field, F32),
             pltpu.VMEM((2, length, length // 2), F32),
@@ -299,12 +329,13 @@
             pltpu.VMEM((above, count, 2, rows, length), F32),
             pltpu.VMEM((count, 2, rows, length), F32),
             pltpu.VMEM((count, 2, rows, length), F32),
+            dma((6,)),
             dma((above,)), dma((above,)),
             dma((above, steps)), dma((above, steps)),
             dma((steps,)), dma((steps,)),
         ],
         compiler_params=pltpu.CompilerParams(
-            collective_id=0, has_side_effects=True, vmem_limit_bytes=40 * 1024 * 1024),
+            collective_id=0, has_side_effects=True, vmem_limit_bytes=60 * 1024 * 1024),
     )(amplitude[0], phase[0], kernel_phase, entry_field[:, 0, 0], cotangent[:, 0], tab)
     return (mine * (1.0 / math.sqrt(angles * count)))[:, None]
 

time: 46.5 us -> 48.4 us (1.041)
  Pallas kernels: 39.6 us -> 46.8 us
  local copies, waits for them, and re-layouts: 5.82 us -> 0 us
  other arithmetic: 0.64 us -> 1.48 us
    pallas_call x1, Pallas kernels: 39.6 us -> 46.8 us  [per_device(): pl.pallas_call(functools.partial(kernel, depth, count), out_shape=jax.Sha...]
    unnamed x12 -> x0, local copies, waits for them, and re-layouts: 5.82 us -> none
    broadcast_in_dim x1, other arithmetic: 0.64 us -> 1.48 us  [per_device(): return (mine * (1.0 / math.sqrt(angles * count)))[:, None]]
where the time goes in v2:
time: 48.4 us; the launch traced here: 48.3 us
  Pallas kernels  46.8 us (97%)
  other arithmetic  1.48 us (3%)
    pallas_call x1, Pallas kernels, per_device(): pl.pallas_call(functools.partial(kernel, depth, count), out_shape=jax.Sha...  46.8 us
    broadcast_in_dim x1, other arithmetic, per_device(): return (mine * (1.0 / math.sqrt(angles * count)))[:, None]  1.48 us

profile of v2, /device:TPU:0, one launch (start us, length us, event | category | flops | bytes accessed | tf_op | source)
XLA Modules:
  0.0 48.3 jit_solution(9470291092499128132)
XLA Ops:
  0.0 46.8 %shard_map.64 = f32[2,32,256]{2,1,0:T(8,128)} custom-call(f32[32,256]{1,0:T(8,128)} %bitcast.10, f32[32,256]{1,0:T(8,128)} %bitcast.11, f32[256,256]{1,0:T(8,128)} %kern_hbm.1, f32[2,256,256]{2,1,0:T(8,128)} %bitcast.8, f32[2,256,256]{2,1,0:T(8,128)} %bitcast.9, bf16[9,256,256]{2,1,0:T(8,128)(2,1)} %constant.4.clone.tab_hbm), custom_call_target="tpu_custom_call" | custom-call | tf_op jit(solution)/shard_map/pallas_call | solution.py:314
  46.8 1.5 %multiply_bitcast_fusion = f32[2,1,32,256]{3,2,1,0:T(8,128)} fusion(f32[2,32,256]{2,1,0:T(8,128)} %shard_map.64), kind=kLoop, calls=%fused_computation | loop fusion | flops 16384 | bytes 131072 | tf_op jit(solution)/shard_map/broadcast_in_dim | solution.py:340

commit v3 on v2

--- a/solution.py
+++ b/solution.py
@@ -74,15 +74,16 @@
 def kernel(
     depth, count, amp_hbm, phase_hbm, kern_hbm, psi_hbm, cot_hbm, tab_hbm, out_ref,
     amp_ref, phase_ref, kern_ref, psi_ref, tab,
-    x_ref, h_ref, tmp_ref, own_ref, t_ref, prod_ref, land_ref, loaded,
-    z_send, z_recv, g_send, g_recv, r_send, r_recv,
+    x_ref, h_ref, tmp_ref, own_ref, t_ref, end_ref, give_ref, got_ref, keep_ref, land_ref, loaded,
+    z_send, z_recv, g_send, g_recv, c_send, c_recv, twin_send, twin_recv, r_send, r_recv,
 ):
     length = kern_ref.shape[0]
     half = length // 2
     rows = amp_ref.shape[0]
-    bits = count.bit_length() - 1
+    chips = count // 2
     d = lax.axis_index("depth")
     me = lax.axis_index("illum")
+    chip, core = me // 2, me % 2
     needed = depth - 1 - d
 
     loads = [
@@ -94,32 +95,24 @@
     for load in loads:
         load.start()
 
-    flip = [(1 << b) * (1 - 2 * (me // (1 << b) % 2)) for b in range(bits)]
-    core = me % 2
-    ahead, other = [], []
-    for r in range(bits - 1):
-        down, up = flip[bits - 1 - r], flip[1 + r]
-        ahead.append(down + core * (up - down))
-        other.append(up + core * (down - up))
-    if bits:
-        ahead.append(flip[0])
+    def near(p):
+        return (chip + p) % chips
 
     def owner(p):
-        order = other if p >= count // 2 else ahead
-        block = me
-        for r in range(bits):
-            if p >> r & 1:
-                block = block + (ahead[r] if r == bits - 1 else order[r])
-        return block
+        if p < chips:
+            return 2 * near(p) + core
+        return 2 * near(p - chips) + 1 - core
 
     def rows_of(p):
         return pl.ds(pl.multiple_of(owner(p) * rows, rows), rows)
 
+    twin = (d, 2 * chip + 1 - core)
     barrier = pltpu.get_barrier_semaphore()
     for o in range(1, depth):
         pl.semaphore_signal(barrier, inc=1, device_id=((d + o) % depth, me), device_id_type=MESH)
-    for r in range(bits):
-        pl.semaphore_signal(barrier, inc=1, device_id=(d, me + ahead[r]), device_id_type=MESH)
+    for p in range(1, chips + 1):
+        peer = (d, owner(p)) if p < chips else twin
+        pl.semaphore_signal(barrier, inc=1, device_id=peer, device_id_type=MESH)
 
     loads[0].wait()
     loads[1].wait()
@@ -127,7 +120,7 @@
     own_ref[0] = amp_ref[...] * cos_t
     own_ref[1] = amp_ref[...] * sin_t
 
-    pl.semaphore_wait(barrier, depth - 1 + bits)
+    pl.semaphore_wait(barrier, depth - 1 + chips)
 
     def z_copy(target):
         return pltpu.make_async_remote_copy(
@@ -145,23 +138,39 @@
 
     post(-1)
 
-    def g_copy(s, r):
-        w = 1 << r
-        return pltpu.make_async_remote_copy(
-            src_ref=t_ref.at[s, pl.ds(0, w)], dst_ref=t_ref.at[s, pl.ds(w, w)],
-            send_sem=g_send.at[s, r], recv_sem=g_recv.at[s, r],
-            device_id=(d, me + ahead[r]), device_id_type=MESH,
+    def g_copy(s, p):
+        return pltpu.make_async_remote_copy(
+            src_ref=t_ref.at[s, 0], dst_ref=t_ref.at[s, chips - p],
+            send_sem=g_send.at[s, p], recv_sem=g_recv.at[s, chips - p],
+            device_id=(d, owner(p)), device_id_type=MESH,
+        )
+
+    def c_copy(s, first, size):
+        which = min(first, 1)
+        return pltpu.make_async_remote_copy(
+            src_ref=t_ref.at[s, pl.ds(first, size)],
+            dst_ref=t_ref.at[s, pl.ds(chips + first, size)],
+            send_sem=c_send.at[s, which], recv_sem=c_recv.at[s, which],
+            device_id=twin, device_id_type=MESH,
         )
 
     def advance(s, step):
-        @pl.when(jnp.logical_and(s >= 0, s < needed))
+        @pl.when(s < needed)
         def _():
             if step == 0:
                 pltpu.make_async_copy(own_ref, t_ref.at[s, 0], z_recv.at[s]).wait()
+                for p in range(1, chips):
+                    g_copy(s, p).start()
+                c_copy(s, 0, 1).start()
+            elif step == 1:
+                for p in range(1, chips):
+                    pltpu.make_async_copy(own_ref, t_ref.at[s, p], g_recv.at[s, p]).wait()
+                if chips > 1:
+                    c_copy(s, 1, chips - 1).start()
             else:
-                g_copy(s, step - 1).wait_recv()
-            if step < bits:
-                g_copy(s, step).start()
+                c_copy(s, 0, 1).wait_recv()
+                if chips > 1:
+                    c_copy(s, 1, chips - 1).wait_recv()
 
     loads[2].wait()
     loads[3].wait()
@@ -217,27 +226,32 @@
             mixed = jnp.concatenate([
                 jnp.concatenate([total[:half, cols], gap[:half, cols]], axis=0),
                 jnp.concatenate([total[half:, cols], gap[half:, cols]], axis=0)], axis=1)
-            ends.append(right(mixed, tab, c))
-        e, o = ends
+            ends.append(mixed)
+        return ends
+
+    def finish(ends):
+        e, o = [right(v, tab, at) for at, v in enumerate(ends)]
         total, gap = e + o, e - o
-        x_ref[0, :, :half] = total[:, :half]
-        x_ref[0, :, half:] = gap[:, :half]
-        x_ref[1, :, :half] = total[:, half:]
-        x_ref[1, :, half:] = gap[:, half:]
-        slot(3)
-
-    slots = max(4, bits + 1 + (bits + 1) % 2)
+        return (
+            jnp.concatenate([total[:, :half], gap[:, :half]], axis=1),
+            jnp.concatenate([total[:, half:], gap[:, half:]], axis=1),
+        )
 
     def slot(q, k):
-        post(q * slots + k)
-        for step in reversed(range(bits + 1)):
-            if (k - step) % 2 == 0:
-                advance(q * (slots // 2) + (k - step) // 2, step)
+        post(q * 4 + k)
+        if k == 0:
+            @pl.when(q == 0)
+            def _():
+                advance(q, 0)
+        elif k == 1:
+            advance(q, 1)
+            advance(q + 1, 0)
+        elif k == 3:
+            advance(q, 2)
 
     def body(q, carry):
-        propagate(functools.partial(slot, q))
-        for k in range(4, slots):
-            slot(q, k)
+        x_ref[0], x_ref[1] = finish(propagate(functools.partial(slot, q)))
+        slot(q, 3)
         for p in range(count):
             at = rows_of(p)
             t_re, t_im = t_ref[q, p, 0], t_ref[q, p, 1]
@@ -247,54 +261,66 @@
         return carry
 
     lax.fori_loop(0, needed, body, 0)
-    propagate(lambda k: post(needed * slots + k))
-
-    @pl.loop(jnp.minimum(needed * slots + 5 - needed, d), d)
+    ends = propagate(lambda k: post(needed * 4 + k))
+    for c in (0, 1):
+        end_ref[c] = ends[c].reshape(chips, 2, rows, length)
+
+    @pl.loop(jnp.minimum(needed * 4 + 4 - needed, d), d)
     def _(target):
         z_copy(target).start()
 
+    def products(to_ref, kind):
+        flat = (chips * rows, length)
+        u_re, u_im = finish([end_ref[c, :, kind].reshape(flat) for c in (0, 1)])
+        p_re, p_im = [psi_ref[c, :, kind].reshape(flat) for c in (0, 1)]
+        shape = (chips, rows, length)
+        to_ref[:, 0] = (u_re * p_re + u_im * p_im).reshape(shape)
+        to_ref[:, 1] = (u_im * p_re - u_re * p_im).reshape(shape)
+
+    def twin_copy(p):
+        at = near(p)
+        return pltpu.make_async_remote_copy(
+            src_ref=give_ref.at[at], dst_ref=got_ref.at[at],
+            send_sem=twin_send.at[p], recv_sem=twin_recv.at[p],
+            device_id=twin, device_id_type=MESH,
+        )
+
+    def sum_copy(p):
+        return pltpu.make_async_remote_copy(
+            src_ref=keep_ref.at[near(p)], dst_ref=land_ref.at[chips - p],
+            send_sem=r_send.at[p], recv_sem=r_recv.at[chips - p],
+            device_id=(d, owner(p)), device_id_type=MESH,
+        )
+
     loads[5].wait()
-
-    def product(p):
-        at = rows_of(p)
-        u_re, u_im = x_ref[0, at], x_ref[1, at]
-        p_re, p_im = psi_ref[0, at], psi_ref[1, at]
-        prod_ref[p, 0] = u_re * p_re + u_im * p_im
-        prod_ref[p, 1] = u_im * p_re - u_re * p_im
-
-    def r_copy(r):
-        w = 1 << r
-        return pltpu.make_async_remote_copy(
-            src_ref=prod_ref.at[pl.ds(w, w)], dst_ref=land_ref.at[pl.ds(w, w)],
-            send_sem=r_send.at[r], recv_sem=r_recv.at[r],
-            device_id=(d, me + ahead[r]), device_id_type=MESH,
-        )
-
-    for p in range(count // 2, count):
-        product(p)
-    if bits:
-        r_copy(bits - 1).start()
-    for p in range(count // 2):
-        product(p)
-    for r in reversed(range(bits)):
-        w = 1 << r
-        r_copy(r).wait_recv()
-        if r:
-            v = w // 2
-            prod_ref[v:w] += land_ref[w + v:2 * w]
-            r_copy(r - 1).start()
-            prod_ref[:v] += land_ref[w:w + v]
-        else:
-            prod_ref[0] += land_ref[1]
-    out_ref[...] = prod_ref[0]
-
-    for r in range(bits):
-        r_copy(r).wait_send()
+    products(give_ref, 1 - core)
+    order = [*range(1, chips), 0]
+    for p in order:
+        twin_copy(p).start()
+    products(keep_ref, core)
+    for p in order:
+        twin_copy(p).wait_recv()
+        if p:
+            keep_ref[near(p)] += got_ref[near(p)]
+            sum_copy(p).start()
+    total = keep_ref[chip] + got_ref[chip]
+    for p in range(1, chips):
+        pltpu.make_async_copy(own_ref, land_ref.at[p], r_recv.at[p]).wait()
+        total = total + land_ref[p]
+    out_ref[...] = total
+
+    for p in range(chips):
+        twin_copy(p).wait_send()
+        if p:
+            sum_copy(p).wait_send()
 
     @pl.loop(0, needed)
     def _(s):
-        for r in range(bits):
-            g_copy(s, r).wait_send()
+        for p in range(1, chips):
+            g_copy(s, p).wait_send()
+        c_copy(s, 0, 1).wait_send()
+        if chips > 1:
+            c_copy(s, 1, chips - 1).wait_send()
 
     @pl.loop(0, d)
     def _(target):
@@ -304,39 +330,44 @@
 def per_device(depth, count, amplitude, phase, kernel_phase, entry_field, cotangent):
     _, rows, length = amplitude.shape
     angles = entry_field.shape[2]
-    assert angles == 1 and amplitude.shape[0] == 1
-    bits = count.bit_length() - 1
-    assert count == 1 << bits
-    above, steps = max(depth - 1, 1), max(bits, 1)
+    assert angles == 1 and amplitude.shape[0] == 1 and count % 2 == 0
+    chips, above = count // 2, max(depth - 1, 1)
     tab = jnp.asarray(tables(length))
     field = (2, length, length)
+    blocks = (2, chips, 2, rows, length)
+    half_sum = (chips, 2, rows, length)
     dma = pltpu.SemaphoreType.DMA
     mine = pl.pallas_call(
         functools.partial(kernel, depth, count),
         out_shape=jax.ShapeDtypeStruct((2, rows, length), F32),
-        in_specs=[pl.BlockSpec(memory_space=pl.ANY)] * 6,
+        in_specs=[pl.BlockSpec(memory_space=pltpu.HBM)] * 6,
         out_specs=pl.BlockSpec(memory_space=pltpu.VMEM),
         scratch_shapes=[
             pltpu.VMEM((rows, length), F32),
             pltpu.VMEM((rows, length), F32),
             pltpu.VMEM((length, length), F32),
-            pltpu.VMEM(field, F32),
+            pltpu.VMEM(blocks, F32),
             pltpu.VMEM(tab.shape, BF16),
             pltpu.VMEM(field, F32),
             pltpu.VMEM(field, F32),
             pltpu.VMEM((2, length, length // 2), F32),
             pltpu.VMEM((2, rows, length), F32),
             pltpu.VMEM((above, count, 2, rows, length), F32),
-            pltpu.VMEM((count, 2, rows, length), F32),
-            pltpu.VMEM((count, 2, rows, length), F32),
+            pltpu.VMEM(blocks, F32),
+            pltpu.VMEM(half_sum, F32),
+            pltpu.VMEM(half_sum, F32),
+            pltpu.VMEM(half_sum, F32),
+            pltpu.VMEM(half_sum, F32),
             dma((6,)),
             dma((above,)), dma((above,)),
-            dma((above, steps)), dma((above, steps)),
-            dma((steps,)), dma((steps,)),
+            dma((above, chips)), dma((above, chips)),
+            dma((above, 2)), dma((above, 2)),
+            dma((chips,)), dma((chips,)), dma((chips,)), dma((chips,)),
         ],
         compiler_params=pltpu.CompilerParams(
-            collective_id=0, has_side_effects=True, vmem_limit_bytes=60 * 1024 * 1024),
-    )(amplitude[0], phase[0], kernel_phase, entry_field[:, 0, 0], cotangent[:, 0], tab)
+            collective_id=0, has_side_effects=True, vmem_limit_bytes=24 * 1024 * 1024),
+    )(amplitude[0], phase[0], kernel_phase,
+      entry_field.reshape(blocks), cotangent[:, 0], tab)
     return (mine * (1.0 / math.sqrt(angles * count)))[:, None]
 
 

time: 48.4 us -> 40.5 us (0.84)
  Pallas kernels: 46.8 us -> 33.6 us
  local copies, waits for them, and re-layouts: 0 us -> 5.82 us
  other arithmetic: 1.48 us -> 0.64 us
    pallas_call x1, Pallas kernels: 46.8 us -> 33.6 us  [per_device(): pl.pallas_call(functools.partial(kernel, depth, count), out_shape=jax.Sha...]
    unnamed x0 -> x12, local copies, waits for them, and re-layouts: none -> 5.82 us
    broadcast_in_dim x1, other arithmetic: 1.48 us -> 0.64 us  [per_device(): return (mine * (1.0 / math.sqrt(angles * count)))[:, None]]
where the time goes in v3:
time: 40.5 us; the launch traced here: 40.1 us
  Pallas kernels  33.6 us (83%)
  local copies, waits for them, and re-layouts  5.82 us (14%)
  other arithmetic  0.64 us (2%)
    pallas_call x1, Pallas kernels, per_device(): pl.pallas_call(functools.partial(kernel, depth, count), out_shape=jax.Sha...  33.6 us
    unnamed x12, local copies, waits for them, and re-layouts  5.82 us

profile of v3, /device:TPU:0, one launch (start us, length us, event | category | flops | bytes accessed | tf_op | source)
XLA Modules:
  0.0 40.1 jit_solution(17357165780754985926)
XLA Ops:
  0.0 0.0 copy-start
  0.0 1.3 %copy-done = bf16[9,256,256]{2,1,0:T(8,128)(2,1)S(1)} copy-done((bf16[9,256,256]{2,1,0:T(8,128)(2,1)S(1)}, bf16[9,256,256]{2,1,0:T(8,128)(2,1)}, u32[]{:S(2)}) %copy-start) | copy-done | bytes 1179672
  1.3 0.0 copy-start.1
  1.3 1.0 %copy-done.1 = f32[2,1,1,256,256]{4,3,2,1,0:T(8,128)S(1)} copy-done((f32[2,1,1,256,256]{4,3,2,1,0:T(8,128)S(1)}, f32[2,1,1,256,256]{4,3,2,1,0:T(8,128)}, u32[]{:S(2)}) %copy-start.1) | copy-done | bytes 524312
  2.3 0.0 copy-start.2
  2.3 1.0 %copy-done.2 = f32[2,1,256,256]{3,2,1,0:T(8,128)S(1)} copy-done((f32[2,1,256,256]{3,2,1,0:T(8,128)S(1)}, f32[2,1,256,256]{3,2,1,0:T(8,128)}, u32[]{:S(2)}) %copy-start.2) | copy-done | bytes 524312
  3.4 0.0 copy-start.3
  3.4 0.9 %copy-done.3 = f32[256,256]{1,0:T(8,128)S(1)} copy-done((f32[256,256]{1,0:T(8,128)S(1)}, f32[256,256]{1,0:T(8,128)}, u32[]{:S(2)}) %copy-start.3) | copy-done | bytes 262168
  4.3 0.0 copy-start.4
  4.3 0.8 %copy-done.4 = f32[1,32,256]{2,1,0:T(8,128)S(1)} copy-done((f32[1,32,256]{2,1,0:T(8,128)S(1)}, f32[1,32,256]{2,1,0:T(8,128)}, u32[]{:S(2)}) %copy-start.4) | copy-done | bytes 32792
  5.1 0.0 copy-start.5
  5.1 0.8 %copy-done.5 = f32[1,32,256]{2,1,0:T(8,128)S(1)} copy-done((f32[1,32,256]{2,1,0:T(8,128)S(1)}, f32[1,32,256]{2,1,0:T(8,128)}, u32[]{:S(2)}) %copy-start.5) | copy-done | bytes 32792
  5.8 33.6 %shard_map.64 = f32[2,32,256]{2,1,0:T(8,128)S(1)} custom-call(f32[32,256]{1,0:T(8,128)S(1)} %bitcast.10, f32[32,256]{1,0:T(8,128)S(1)} %bitcast.11, f32[256,256]{1,0:T(8,128)S(1)} %copy-done.3, f32[2,4,2,32,256]{4,3,2,1,0:T(8,128)S(1)} %bitcast.8, f32[2,256,256]{2,1,0:T(8,128)S(1)} %bitcast.9, bf16[9,256,256]{2,1,0:T(8,128)(2,1)S(1)} %copy-done), custom_call_target="tpu_custom_call" | custom-call | tf_op jit(solution)/shard_map/pallas_call | solution.py:340
  39.4 0.6 %multiply_bitcast_fusion = f32[2,1,32,256]{3,2,1,0:T(8,128)} fusion(f32[2,32,256]{2,1,0:T(8,128)S(1)} %shard_map.64), kind=kLoop, calls=%fused_computation | loop fusion | flops 16384 | bytes 131072 | tf_op jit(solution)/shard_map/broadcast_in_dim | solution.py:371
Async XLA Ops:
  0.0 1.3 %copy-start = (bf16[9,256,256]{2,1,0:T(8,128)(2,1)S(1)}, bf16[9,256,256]{2,1,0:T(8,128)(2,1)}, u32[]{:S(2)}) copy-start(bf16[9,256,256]{2,1,0:T(8,128)(2,1)} %constant.4.clone.tab_hbm) | copy-start | bytes 3538948
  1.3 1.0 %copy-start.1 = (f32[2,1,1,256,256]{4,3,2,1,0:T(8,128)S(1)}, f32[2,1,1,256,256]{4,3,2,1,0:T(8,128)}, u32[]{:S(2)}) copy-start(f32[2,1,1,256,256]{4,3,2,1,0:T(8,128)} %param.9) | copy-start | bytes 1572868
  2.3 1.0 %copy-start.2 = (f32[2,1,256,256]{3,2,1,0:T(8,128)S(1)}, f32[2,1,256,256]{3,2,1,0:T(8,128)}, u32[]{:S(2)}) copy-start(f32[2,1,256,256]{3,2,1,0:T(8,128)} %param.10) | copy-start | bytes 1572868
  3.4 0.9 %copy-start.3 = (f32[256,256]{1,0:T(8,128)S(1)}, f32[256,256]{1,0:T(8,128)}, u32[]{:S(2)}) copy-start(f32[256,256]{1,0:T(8,128)} %kern_hbm.1) | copy-start | bytes 786436
  4.3 0.8 %copy-start.4 = (f32[1,32,256]{2,1,0:T(8,128)S(1)}, f32[1,32,256]{2,1,0:T(8,128)}, u32[]{:S(2)}) copy-start(f32[1,32,256]{2,1,0:T(8,128)} %param.6) | copy-start | bytes 98308
  5.1 0.8 %copy-start.5 = (f32[1,32,256]{2,1,0:T(8,128)S(1)}, f32[1,32,256]{2,1,0:T(8,128)}, u32[]{:S(2)}) copy-start(f32[1,32,256]{2,1,0:T(8,128)} %param.7) | copy-start | bytes 98308

commit v4 on v3

--- a/solution.py
+++ b/solution.py
@@ -23,18 +23,22 @@
 
 def tables(length):
     half = length // 2
-    out = []
+    lefts = []
     for odd in (0, 1):
         k = 2 * np.arange(half)[:, None] + odd
         angle = (k * np.arange(half)[None, :] % length) * (2.0 * np.pi / length)
         c, s = np.cos(angle), np.sin(angle)
-        out.append(np.block([[c, s], [-s, c]]))
-    out += [out[0].T, out[1].T]
+        lefts.append(np.block([[c, s], [-s, c]]))
+    lefts += [lefts[0].T, lefts[1].T]
     perm = np.concatenate([np.arange(0, length, 2), np.arange(1, length, 2)])
     shuffle = np.zeros((length, length))
     shuffle[perm, np.arange(length)] = 1.0
-    stacked = sum([halves(m) for m in out], [])
-    return np.stack(stacked + [shuffle.astype(ml_dtypes.bfloat16)])
+    wide, tall = [], []
+    for high, low in map(halves, lefts):
+        wide.append(np.concatenate([high, high, low], axis=1))
+    for high, low in map(halves, lefts):
+        tall.append(np.concatenate([high, high, low], axis=0))
+    return np.stack(wide), np.stack(tall), shuffle.astype(ml_dtypes.bfloat16)
 
 
 def sincos(x):
@@ -61,19 +65,17 @@
 
 def right(v, tab, at):
     high, low = split(v)
-    w_high, w_low = tab[2 * at], tab[2 * at + 1]
-    return dot(low, w_high) + dot(high, w_low) + dot(high, w_high)
+    return dot(jnp.concatenate([high, low, high], axis=1), tab[at])
 
 
 def left(v, tab, at):
     high, low = split(v)
-    w_high, w_low = tab[2 * at], tab[2 * at + 1]
-    return dot(w_high, low) + dot(w_low, high) + dot(w_high, high)
+    return dot(tab[at], jnp.concatenate([high, low, high], axis=0))
 
 
 def kernel(
-    depth, count, amp_hbm, phase_hbm, kern_hbm, psi_hbm, cot_hbm, tab_hbm, out_ref,
-    amp_ref, phase_ref, kern_ref, psi_ref, tab,
+    depth, count, amp_hbm, phase_hbm, kern_hbm, psi_hbm, cot_hbm, wide_hbm, tall_hbm, shuffle_hbm, out_ref,
+    amp_ref, phase_ref, kern_ref, psi_ref, wide, tall, shuffle_ref,
     x_ref, h_ref, tmp_ref, own_ref, t_ref, end_ref, give_ref, got_ref, keep_ref, land_ref, loaded,
     z_send, z_recv, g_send, g_recv, c_send, c_recv, twin_send, twin_recv, r_send, r_recv,
 ):
@@ -90,7 +92,8 @@
         pltpu.make_async_copy(source, target, loaded.at[i])
         for i, (source, target) in enumerate([
             (amp_hbm, amp_ref), (phase_hbm, phase_ref), (kern_hbm, kern_ref),
-            (tab_hbm, tab), (cot_hbm, x_ref), (psi_hbm, psi_ref)])
+            (shuffle_hbm, shuffle_ref), (cot_hbm, x_ref), (tall_hbm, tall),
+            (wide_hbm, wide), (psi_hbm, psi_ref)])
     ]
     for load in loads:
         load.start()
@@ -178,7 +181,7 @@
     first, rest = split(phase)
     rest = phase - first.astype(F32)
     second, third = split(rest)
-    shuffle = tab[8]
+    shuffle = shuffle_ref[...]
     moved = (dot(third, shuffle) + dot(second, shuffle)) + dot(first, shuffle)
     tmp_ref[0], tmp_ref[1] = moved[:, :half], moved[:, half:]
     scale = 1.0 / (length * length)
@@ -189,7 +192,8 @@
             h_ref[(0, *at)] = cos_h * scale
             h_ref[(1, *at)] = sin_h * scale
 
-    loads[4].wait()
+    for load in loads[4:7]:
+        load.wait()
 
     def propagate(slot):
         re, im = x_ref[0], x_ref[1]
@@ -197,7 +201,7 @@
         for sign, at in ((1, 2), (-1, 3)):
             mixed = jnp.concatenate(
                 [v[:, :half] + sign * v[:, half:] for v in (re, im)], axis=1)
-            parts.append(right(mixed, tab, at))
+            parts.append(right(mixed, tall, at))
         slot(0)
         even, odd = parts
         back = []
@@ -208,7 +212,7 @@
                     v[:half, c * half:(c + 1) * half] + sign * v[half:, c * half:(c + 1) * half]
                     for v in (even, odd)], axis=1)
                 for c in (0, 1)], axis=0)
-            freq = left(stack, tab, at)
+            freq = left(stack, wide, at)
             f_re, f_im = freq[:half], freq[half:]
             h_re = h_ref[0, at * half:(at + 1) * half]
             h_im = h_ref[1, at * half:(at + 1) * half]
@@ -216,7 +220,7 @@
                 [f_re * h_re + f_im * h_im, f_im * h_re - f_re * h_im], axis=0))
         slot(1)
         for at in (0, 1):
-            back.append(left(mixes[at], tab, 2 + at))
+            back.append(left(mixes[at], wide, 2 + at))
         slot(2)
         e, o = back
         total, gap = e + o, e - o
@@ -230,7 +234,7 @@
         return ends
 
     def finish(ends):
-        e, o = [right(v, tab, at) for at, v in enumerate(ends)]
+        e, o = [right(v, tall, at) for at, v in enumerate(ends)]
         total, gap = e + o, e - o
         return (
             jnp.concatenate([total[:, :half], gap[:, :half]], axis=1),
@@ -292,7 +296,7 @@
             device_id=(d, owner(p)), device_id_type=MESH,
         )
 
-    loads[5].wait()
+    loads[7].wait()
     products(give_ref, 1 - core)
     order = [*range(1, chips), 0]
     for p in order:
@@ -332,7 +336,7 @@
     angles = entry_field.shape[2]
     assert angles == 1 and amplitude.shape[0] == 1 and count % 2 == 0
     chips, above = count // 2, max(depth - 1, 1)
-    tab = jnp.asarray(tables(length))
+    wide, tall, shuffle = map(jnp.asarray, tables(length))
     field = (2, length, length)
     blocks = (2, chips, 2, rows, length)
     half_sum = (chips, 2, rows, length)
@@ -340,14 +344,16 @@
     mine = pl.pallas_call(
         functools.partial(kernel, depth, count),
         out_shape=jax.ShapeDtypeStruct((2, rows, length), F32),
-        in_specs=[pl.BlockSpec(memory_space=pltpu.HBM)] * 6,
+        in_specs=[pl.BlockSpec(memory_space=pltpu.HBM)] * 8,
         out_specs=pl.BlockSpec(memory_space=pltpu.VMEM),
         scratch_shapes=[
             pltpu.VMEM((rows, length), F32),
             pltpu.VMEM((rows, length), F32),
             pltpu.VMEM((length, length), F32),
             pltpu.VMEM(blocks, F32),
-            pltpu.VMEM(tab.shape, BF16),
+            pltpu.VMEM(wide.shape, BF16),
+            pltpu.VMEM(tall.shape, BF16),
+            pltpu.VMEM(shuffle.shape, BF16),
             pltpu.VMEM(field, F32),
             pltpu.VMEM(field, F32),
             pltpu.VMEM((2, length, length // 2), F32),
@@ -358,16 +364,16 @@
             pltpu.VMEM(half_sum, F32),
             pltpu.VMEM(half_sum, F32),
             pltpu.VMEM(half_sum, F32),
-            dma((6,)),
+            dma((8,)),
             dma((above,)), dma((above,)),
             dma((above, chips)), dma((above, chips)),
             dma((above, 2)), dma((above, 2)),
             dma((chips,)), dma((chips,)), dma((chips,)), dma((chips,)),
         ],
         compiler_params=pltpu.CompilerParams(
-            collective_id=0, has_side_effects=True, vmem_limit_bytes=24 * 1024 * 1024),
+            collective_id=0, has_side_effects=True, vmem_limit_bytes=60 * 1024 * 1024),
     )(amplitude[0], phase[0], kernel_phase,
-      entry_field.reshape(blocks), cotangent[:, 0], tab)
+      entry_field.reshape(blocks), cotangent[:, 0], wide, tall, shuffle)
     return (mine * (1.0 / math.sqrt(angles * count)))[:, None]
 
 

time: 40.5 us -> 35.4 us (0.87)
  local copies, waits for them, and re-layouts: 5.82 us -> 0 us
  other arithmetic: 0.64 us -> 1.48 us
    unnamed x12 -> x0, local copies, waits for them, and re-layouts: 5.82 us -> none
    broadcast_in_dim x1, other arithmetic: 0.64 us -> 1.48 us  [per_device(): return (mine * (1.0 / math.sqrt(angles * count)))[:, None]]
where the time goes in v4:
time: 35.4 us; the launch traced here: 35.3 us
  Pallas kernels  33.8 us (95%)
  other arithmetic  1.48 us (4%)
    pallas_call x1, Pallas kernels, per_device(): pl.pallas_call(functools.partial(kernel, depth, count), out_shape=jax.Sha...  33.8 us
    broadcast_in_dim x1, other arithmetic, per_device(): return (mine * (1.0 / math.sqrt(angles * count)))[:, None]  1.48 us

profile of v4, /device:TPU:0, one launch (start us, length us, event | category | flops | bytes accessed | tf_op | source)
XLA Modules:
  0.0 35.3 jit_solution(2874135167123920346)
XLA Ops:
  0.0 33.8 %shard_map.82 = f32[2,32,256]{2,1,0:T(8,128)} custom-call(f32[32,256]{1,0:T(8,128)} %bitcast.10, f32[32,256]{1,0:T(8,128)} %bitcast.11, f32[256,256]{1,0:T(8,128)} %kern_hbm.1, f32[2,4,2,32,256]{4,3,2,1,0:T(8,128)} %bitcast.8, f32[2,256,256]{2,1,0:T(8,128)} %bitcast.9, bf16[4,256,768]{2,1,0:T(8,128)(2,1)} %constant.8.clone.wide_hbm, ...), custom_call_target="tpu_custom_call" | custom-call | tf_op jit(solution)/shard_map/pallas_call | solution.py:344
  33.8 1.5 %multiply_bitcast_fusion = f32[2,1,32,256]{3,2,1,0:T(8,128)} fusion(f32[2,32,256]{2,1,0:T(8,128)} %shard_map.82), kind=kLoop, calls=%fused_computation | loop fusion | flops 16384 | bytes 131072 | tf_op jit(solution)/shard_map/broadcast_in_dim | solution.py:377

commit v5 on v4

--- a/solution.py
+++ b/solution.py
@@ -106,9 +106,6 @@
             return 2 * near(p) + core
         return 2 * near(p - chips) + 1 - core
 
-    def rows_of(p):
-        return pl.ds(pl.multiple_of(owner(p) * rows, rows), rows)
-
     twin = (d, 2 * chip + 1 - core)
     barrier = pltpu.get_barrier_semaphore()
     for o in range(1, depth):
@@ -127,7 +124,7 @@
 
     def z_copy(target):
         return pltpu.make_async_remote_copy(
-            src_ref=own_ref, dst_ref=t_ref.at[needed, 0],
+            src_ref=own_ref, dst_ref=t_ref.at[needed, chip, core],
             send_sem=z_send.at[target], recv_sem=z_recv.at[needed],
             device_id=(target, me), device_id_type=MESH,
         )
@@ -143,37 +140,40 @@
 
     def g_copy(s, p):
         return pltpu.make_async_remote_copy(
-            src_ref=t_ref.at[s, 0], dst_ref=t_ref.at[s, chips - p],
+            src_ref=t_ref.at[s, chip, core], dst_ref=t_ref.at[s, chip, core],
             send_sem=g_send.at[s, p], recv_sem=g_recv.at[s, chips - p],
             device_id=(d, owner(p)), device_id_type=MESH,
         )
 
-    def c_copy(s, first, size):
-        which = min(first, 1)
-        return pltpu.make_async_remote_copy(
-            src_ref=t_ref.at[s, pl.ds(first, size)],
-            dst_ref=t_ref.at[s, pl.ds(chips + first, size)],
-            send_sem=c_send.at[s, which], recv_sem=c_recv.at[s, which],
+    def c_copy(s, p):
+        block = t_ref.at[s, near(p), core]
+        return pltpu.make_async_remote_copy(
+            src_ref=block, dst_ref=block,
+            send_sem=c_send.at[s, p], recv_sem=c_recv.at[s, p],
             device_id=twin, device_id_type=MESH,
         )
 
-    def advance(s, step):
+    def landed(s, p, sem):
+        pltpu.make_async_copy(own_ref, t_ref.at[s, near(p), core], sem).wait()
+
+    def spread(s):
         @pl.when(s < needed)
         def _():
-            if step == 0:
-                pltpu.make_async_copy(own_ref, t_ref.at[s, 0], z_recv.at[s]).wait()
-                for p in range(1, chips):
-                    g_copy(s, p).start()
-                c_copy(s, 0, 1).start()
-            elif step == 1:
-                for p in range(1, chips):
-                    pltpu.make_async_copy(own_ref, t_ref.at[s, p], g_recv.at[s, p]).wait()
-                if chips > 1:
-                    c_copy(s, 1, chips - 1).start()
-            else:
-                c_copy(s, 0, 1).wait_recv()
-                if chips > 1:
-                    c_copy(s, 1, chips - 1).wait_recv()
+            landed(s, 0, z_recv.at[s])
+            for p in range(1, chips):
+                g_copy(s, p).start()
+            c_copy(s, 0).start()
+
+    def pass_on(s):
+        @pl.when(s < needed)
+        def _():
+            for p in range(1, chips):
+                landed(s, p, g_recv.at[s, p])
+                c_copy(s, p).start()
+
+    def arrived(s):
+        for p in range(chips):
+            c_copy(s, p).wait_recv()
 
     loads[2].wait()
     loads[3].wait()
@@ -195,8 +195,7 @@
     for load in loads[4:7]:
         load.wait()
 
-    def propagate(slot):
-        re, im = x_ref[0], x_ref[1]
+    def propagate(re, im, slot):
         parts = []
         for sign, at in ((1, 2), (-1, 3)):
             mixed = jnp.concatenate(
@@ -224,14 +223,12 @@
         slot(2)
         e, o = back
         total, gap = e + o, e - o
-        ends = []
         for c in (0, 1):
             cols = slice(c * half, (c + 1) * half)
             mixed = jnp.concatenate([
                 jnp.concatenate([total[:half, cols], gap[:half, cols]], axis=0),
                 jnp.concatenate([total[half:, cols], gap[half:, cols]], axis=0)], axis=1)
-            ends.append(mixed)
-        return ends
+            end_ref[c] = mixed.reshape(chips, 2, rows, length)
 
     def finish(ends):
         e, o = [right(v, tall, at) for at, v in enumerate(ends)]
@@ -241,37 +238,33 @@
             jnp.concatenate([total[:, half:], gap[:, half:]], axis=1),
         )
 
-    def slot(q, k):
-        post(q * 4 + k)
+    def first_slot(k):
+        post(k)
         if k == 0:
-            @pl.when(q == 0)
-            def _():
-                advance(q, 0)
+            spread(0)
         elif k == 1:
-            advance(q, 1)
-            advance(q + 1, 0)
-        elif k == 3:
-            advance(q, 2)
-
-    def body(q, carry):
-        x_ref[0], x_ref[1] = finish(propagate(functools.partial(slot, q)))
-        slot(q, 3)
-        for p in range(count):
-            at = rows_of(p)
-            t_re, t_im = t_ref[q, p, 0], t_ref[q, p, 1]
-            u_re, u_im = x_ref[0, at], x_ref[1, at]
-            x_ref[0, at] = u_re * t_re + u_im * t_im
-            x_ref[1, at] = u_im * t_re - u_re * t_im
-        return carry
-
-    lax.fori_loop(0, needed, body, 0)
-    ends = propagate(lambda k: post(needed * 4 + k))
-    for c in (0, 1):
-        end_ref[c] = ends[c].reshape(chips, 2, rows, length)
-
-    @pl.loop(jnp.minimum(needed * 4 + 4 - needed, d), d)
+            pass_on(0)
+            spread(1)
+
+    propagate(x_ref[0], x_ref[1], first_slot)
+
+    @pl.loop(jnp.clip(4 - needed, 0, d), d)
     def _(target):
         z_copy(target).start()
+
+    def body(q, carry):
+        def slot(k):
+            if k == 1:
+                pass_on(q + 1)
+                spread(q + 2)
+
+        u_re, u_im = finish([end_ref[c].reshape(length, length) for c in (0, 1)])
+        arrived(q)
+        t_re, t_im = [t_ref[q, :, :, c].reshape(length, length) for c in (0, 1)]
+        propagate(u_re * t_re + u_im * t_im, u_im * t_re - u_re * t_im, slot)
+        return carry
+
+    lax.fori_loop(0, needed, body, 0)
 
     def products(to_ref, kind):
         flat = (chips * rows, length)
@@ -320,11 +313,10 @@
 
     @pl.loop(0, needed)
     def _(s):
-        for p in range(1, chips):
-            g_copy(s, p).wait_send()
-        c_copy(s, 0, 1).wait_send()
-        if chips > 1:
-            c_copy(s, 1, chips - 1).wait_send()
+        for p in range(chips):
+            c_copy(s, p).wait_send()
+            if p:
+                g_copy(s, p).wait_send()
 
     @pl.loop(0, d)
     def _(target):
@@ -358,7 +350,7 @@
             pltpu.VMEM(field, F32),
             pltpu.VMEM((2, length, length // 2), F32),
             pltpu.VMEM((2, rows, length), F32),
-            pltpu.VMEM((above, count, 2, rows, length), F32),
+            pltpu.VMEM((above, chips, 2, 2, rows, length), F32),
             pltpu.VMEM(blocks, F32),
             pltpu.VMEM(half_sum, F32),
             pltpu.VMEM(half_sum, F32),
@@ -367,7 +359,7 @@
             dma((8,)),
             dma((above,)), dma((above,)),
             dma((above, chips)), dma((above, chips)),
-            dma((above, 2)), dma((above, 2)),
+            dma((above, chips)), dma((above, chips)),
             dma((chips,)), dma((chips,)), dma((chips,)), dma((chips,)),
         ],
         compiler_params=pltpu.CompilerParams(

time: 35.4 us -> 35.4 us (level)
  no operation moved by 1% of the time
where the time goes in v5:
time: 35.4 us; the launch traced here: 35.3 us
  Pallas kernels  33.8 us (95%)
  other arithmetic  1.48 us (4%)
    pallas_call x1, Pallas kernels, per_device(): pl.pallas_call(functools.partial(kernel, depth, count), out_shape=jax.Sha...  33.8 us
    broadcast_in_dim x1, other arithmetic, per_device(): return (mine * (1.0 / math.sqrt(angles * count)))[:, None]  1.48 us

profile of v5, /device:TPU:0, one launch (start us, length us, event | category | flops | bytes accessed | tf_op | source)
XLA Modules:
  0.0 35.3 jit_solution(5868825687679377910)
XLA Ops:
  0.0 33.8 %shard_map.82 = f32[2,32,256]{2,1,0:T(8,128)} custom-call(f32[32,256]{1,0:T(8,128)} %bitcast.10, f32[32,256]{1,0:T(8,128)} %bitcast.11, f32[256,256]{1,0:T(8,128)} %kern_hbm.1, f32[2,4,2,32,256]{4,3,2,1,0:T(8,128)} %bitcast.8, f32[2,256,256]{2,1,0:T(8,128)} %bitcast.9, bf16[4,256,768]{2,1,0:T(8,128)(2,1)} %constant.8.clone.wide_hbm, ...), custom_call_target="tpu_custom_call" | custom-call | tf_op jit(solution)/shard_map/pallas_call | solution.py:336
  33.8 1.5 %multiply_bitcast_fusion = f32[2,1,32,256]{3,2,1,0:T(8,128)} fusion(f32[2,32,256]{2,1,0:T(8,128)} %shard_map.82), kind=kLoop, calls=%fused_computation | loop fusion | flops 16384 | bytes 131072 | tf_op jit(solution)/shard_map/broadcast_in_dim | solution.py:369

commit v6 on v5

--- a/solution.py
+++ b/solution.py
@@ -122,25 +122,30 @@
 
     pl.semaphore_wait(barrier, depth - 1 + chips)
 
-    def z_copy(target):
-        return pltpu.make_async_remote_copy(
-            src_ref=own_ref, dst_ref=t_ref.at[needed, chip, core],
-            send_sem=z_send.at[target], recv_sem=z_recv.at[needed],
+    def z_copy(target, c):
+        return pltpu.make_async_remote_copy(
+            src_ref=own_ref.at[c], dst_ref=t_ref.at[needed, chip, core, c],
+            send_sem=z_send.at[target, c], recv_sem=z_recv.at[needed, c],
             device_id=(target, me), device_id_type=MESH,
         )
+
+    def z_start(target):
+        z_copy(target, 0).start()
+        z_copy(target, 1).start()
 
     def post(g):
         target = g + 1 - needed
 
         @pl.when(jnp.logical_and(target >= 0, target < d))
         def _():
-            z_copy(target).start()
+            z_start(target)
 
     post(-1)
 
-    def g_copy(s, p):
-        return pltpu.make_async_remote_copy(
-            src_ref=t_ref.at[s, chip, core], dst_ref=t_ref.at[s, chip, core],
+    def g_copy(s, p, part=slice(None)):
+        block = t_ref.at[s, chip, core, part]
+        return pltpu.make_async_remote_copy(
+            src_ref=block, dst_ref=block,
             send_sem=g_send.at[s, p], recv_sem=g_recv.at[s, chips - p],
             device_id=(d, owner(p)), device_id_type=MESH,
         )
@@ -153,23 +158,29 @@
             device_id=twin, device_id_type=MESH,
         )
 
-    def landed(s, p, sem):
-        pltpu.make_async_copy(own_ref, t_ref.at[s, near(p), core], sem).wait()
-
     def spread(s):
         @pl.when(s < needed)
         def _():
-            landed(s, 0, z_recv.at[s])
-            for p in range(1, chips):
-                g_copy(s, p).start()
+            for c in (0, 1):
+                pltpu.make_async_copy(
+                    own_ref.at[c], t_ref.at[s, chip, core, c], z_recv.at[s, c]).wait()
+                for p in range(1, chips):
+                    g_copy(s, p, pl.ds(c, 1)).start()
             c_copy(s, 0).start()
 
-    def pass_on(s):
+    def pass_on(s, p):
         @pl.when(s < needed)
         def _():
-            for p in range(1, chips):
-                landed(s, p, g_recv.at[s, p])
-                c_copy(s, p).start()
+            pltpu.make_async_copy(own_ref, t_ref.at[s, near(p), core], g_recv.at[s, p]).wait()
+            c_copy(s, p).start()
+
+    def pass_all(s):
+        for p in range(1, chips):
+            pass_on(s, p)
+            if p == 1:
+                spread(s + 1)
+        if chips == 1:
+            spread(s + 1)
 
     def arrived(s):
         for p in range(chips):
@@ -243,20 +254,18 @@
         if k == 0:
             spread(0)
         elif k == 1:
-            pass_on(0)
-            spread(1)
+            pass_all(0)
 
     propagate(x_ref[0], x_ref[1], first_slot)
 
     @pl.loop(jnp.clip(4 - needed, 0, d), d)
     def _(target):
-        z_copy(target).start()
+        z_start(target)
 
     def body(q, carry):
         def slot(k):
             if k == 1:
-                pass_on(q + 1)
-                spread(q + 2)
+                pass_all(q + 1)
 
         u_re, u_im = finish([end_ref[c].reshape(length, length) for c in (0, 1)])
         arrived(q)
@@ -304,7 +313,7 @@
     for p in range(1, chips):
         pltpu.make_async_copy(own_ref, land_ref.at[p], r_recv.at[p]).wait()
         total = total + land_ref[p]
-    out_ref[...] = total
+    out_ref[:, 0] = total * (1.0 / math.sqrt(count))
 
     for p in range(chips):
         twin_copy(p).wait_send()
@@ -320,7 +329,8 @@
 
     @pl.loop(0, d)
     def _(target):
-        z_copy(target).wait_send()
+        z_copy(target, 0).wait_send()
+        z_copy(target, 1).wait_send()
 
 
 def per_device(depth, count, amplitude, phase, kernel_phase, entry_field, cotangent):
@@ -333,9 +343,9 @@
     blocks = (2, chips, 2, rows, length)
     half_sum = (chips, 2, rows, length)
     dma = pltpu.SemaphoreType.DMA
-    mine = pl.pallas_call(
+    return pl.pallas_call(
         functools.partial(kernel, depth, count),
-        out_shape=jax.ShapeDtypeStruct((2, rows, length), F32),
+        out_shape=jax.ShapeDtypeStruct((2, 1, rows, length), F32),
         in_specs=[pl.BlockSpec(memory_space=pltpu.HBM)] * 8,
         out_specs=pl.BlockSpec(memory_space=pltpu.VMEM),
         scratch_shapes=[
@@ -357,7 +367,7 @@
             pltpu.VMEM(half_sum, F32),
             pltpu.VMEM(half_sum, F32),
             dma((8,)),
-            dma((above,)), dma((above,)),
+            dma((above, 2)), dma((above, 2)),
             dma((above, chips)), dma((above, chips)),
             dma((above, chips)), dma((above, chips)),
             dma((chips,)), dma((chips,)), dma((chips,)), dma((chips,)),
@@ -366,7 +376,6 @@
             collective_id=0, has_side_effects=True, vmem_limit_bytes=60 * 1024 * 1024),
     )(amplitude[0], phase[0], kernel_phase,
       entry_field.reshape(blocks), cotangent[:, 0], wide, tall, shuffle)
-    return (mine * (1.0 / math.sqrt(angles * count)))[:, None]
 
 
 def solution(mesh):

time: 35.4 us -> 34.6 us (0.977)
  other arithmetic: 1.48 us -> 0 us
  local copies, waits for them, and re-layouts: 0 us -> 1.47 us
  Pallas kernels: 33.8 us -> 32.9 us
    broadcast_in_dim x1 -> x0, other arithmetic: 1.48 us -> none  [per_device(): return (mine * (1.0 / math.sqrt(angles * count)))[:, None]]
    unnamed x0 -> x1, local copies, waits for them, and re-layouts: none -> 1.47 us
    pallas_call x1, Pallas kernels: 33.8 us -> 32.9 us  [per_device(): pl.pallas_call(functools.partial(kernel, depth, count), out_shape=jax.Sha...]
where the time goes in v6:
time: 34.6 us; the launch traced here: 34.4 us
  Pallas kernels  32.9 us (95%)
  local copies, waits for them, and re-layouts  1.47 us (4%)
    pallas_call x1, Pallas kernels, per_device(): pl.pallas_call(functools.partial(kernel, depth, count), out_shape=jax.Sha...  32.9 us
    unnamed x1, local copies, waits for them, and re-layouts  1.47 us

profile of v6, /device:TPU:0, one launch (start us, length us, event | category | flops | bytes accessed | tf_op | source)
XLA Modules:
  0.0 34.4 jit_solution(1365434007131316360)
XLA Ops:
  0.0 32.9 %shard_map.82 = f32[2,1,32,256]{3,2,1,0:T(8,128)} custom-call(f32[32,256]{1,0:T(8,128)} %bitcast.6, f32[32,256]{1,0:T(8,128)} %bitcast.7, f32[256,256]{1,0:T(8,128)} %kern_hbm.1, f32[2,4,2,32,256]{4,3,2,1,0:T(8,128)} %bitcast.4, f32[2,256,256]{2,1,0:T(8,128)} %bitcast.5, bf16[4,256,768]{2,1,0:T(8,128)(2,1)} %constant.6.clone.wide_hbm, ...), custom_call_target="tpu_custom_call" | custom-call | tf_op jit(solution)/shard_map/pallas_call | solution.py:346
  32.9 1.5 %copy.10 = f32[2,1,32,256]{3,2,1,0:T(8,128)} copy(f32[2,1,32,256]{3,2,1,0:T(8,128)} %shard_map.82) | data formatting | bytes 131072

commit v7 on v6

--- a/solution.py
+++ b/solution.py
@@ -77,7 +77,7 @@
     depth, count, amp_hbm, phase_hbm, kern_hbm, psi_hbm, cot_hbm, wide_hbm, tall_hbm, shuffle_hbm, out_ref,
     amp_ref, phase_ref, kern_ref, psi_ref, wide, tall, shuffle_ref,
     x_ref, h_ref, tmp_ref, own_ref, t_ref, end_ref, give_ref, got_ref, keep_ref, land_ref, loaded,
-    z_send, z_recv, g_send, g_recv, c_send, c_recv, twin_send, twin_recv, r_send, r_recv,
+    z_send, z_recv, n_send, g_send, g_recv, c_send, c_recv, twin_send, twin_recv, r_send, r_recv,
 ):
     length = kern_ref.shape[0]
     half = length // 2
@@ -108,11 +108,22 @@
 
     twin = (d, 2 * chip + 1 - core)
     barrier = pltpu.get_barrier_semaphore()
-    for o in range(1, depth):
-        pl.semaphore_signal(barrier, inc=1, device_id=((d + o) % depth, me), device_id_type=MESH)
-    for p in range(1, chips + 1):
-        peer = (d, owner(p)) if p < chips else twin
-        pl.semaphore_signal(barrier, inc=1, device_id=peer, device_id_type=MESH)
+
+    def greet(plane, block):
+        pl.semaphore_signal(barrier, inc=1, device_id=(plane, block), device_id_type=MESH)
+
+    @pl.loop(d + 1, depth)
+    def _(plane):
+        greet(plane, me)
+
+    for p in range(1, chips):
+        greet(d, owner(p))
+
+        @pl.when(d < depth - 1)
+        def _():
+            greet(d + 1, owner(p))
+
+    greet(*twin)
 
     loads[0].wait()
     loads[1].wait()
@@ -120,7 +131,7 @@
     own_ref[0] = amp_ref[...] * cos_t
     own_ref[1] = amp_ref[...] * sin_t
 
-    pl.semaphore_wait(barrier, depth - 1 + chips)
+    pl.semaphore_wait(barrier, d + (chips - 1) * jnp.minimum(d, 1) + chips)
 
     def z_copy(target, c):
         return pltpu.make_async_remote_copy(
@@ -129,12 +140,28 @@
             device_id=(target, me), device_id_type=MESH,
         )
 
+    def next_copy(p):
+        return pltpu.make_async_remote_copy(
+            src_ref=own_ref, dst_ref=t_ref.at[needed, chip, core],
+            send_sem=n_send.at[p], recv_sem=g_recv.at[needed, (chips - p) % chips],
+            device_id=(d - 1, owner(p)), device_id_type=MESH,
+        )
+
     def z_start(target):
-        z_copy(target, 0).start()
-        z_copy(target, 1).start()
+        @pl.when(target < d - 1)
+        def _():
+            z_copy(target, 0).start()
+            z_copy(target, 1).start()
+
+        @pl.when(target == d - 1)
+        def _():
+            for p in range(chips):
+                next_copy(p).start()
+
+    lead = 1 - jnp.minimum(needed, 1)
 
     def post(g):
-        target = g + 1 - needed
+        target = g + lead
 
         @pl.when(jnp.logical_and(target >= 0, target < d))
         def _():
@@ -159,7 +186,7 @@
         )
 
     def spread(s):
-        @pl.when(s < needed)
+        @pl.when(s < needed - 1)
         def _():
             for c in (0, 1):
                 pltpu.make_async_copy(
@@ -169,18 +196,16 @@
             c_copy(s, 0).start()
 
     def pass_on(s, p):
-        @pl.when(s < needed)
+        @pl.when(s < needed if p else s == needed - 1)
         def _():
             pltpu.make_async_copy(own_ref, t_ref.at[s, near(p), core], g_recv.at[s, p]).wait()
             c_copy(s, p).start()
 
     def pass_all(s):
-        for p in range(1, chips):
+        for p in [*range(1, chips), 0]:
             pass_on(s, p)
-            if p == 1:
+            if p == min(1, chips - 1):
                 spread(s + 1)
-        if chips == 1:
-            spread(s + 1)
 
     def arrived(s):
         for p in range(chips):
@@ -258,7 +283,7 @@
 
     propagate(x_ref[0], x_ref[1], first_slot)
 
-    @pl.loop(jnp.clip(4 - needed, 0, d), d)
+    @pl.loop(jnp.minimum(3 + lead, d), d)
     def _(target):
         z_start(target)
 
@@ -324,13 +349,21 @@
     def _(s):
         for p in range(chips):
             c_copy(s, p).wait_send()
-            if p:
-                g_copy(s, p).wait_send()
-
-    @pl.loop(0, d)
+
+    @pl.loop(0, jnp.maximum(needed - 1, 0))
+    def _(s):
+        for p in range(1, chips):
+            g_copy(s, p).wait_send()
+
+    @pl.loop(0, jnp.maximum(d - 1, 0))
     def _(target):
         z_copy(target, 0).wait_send()
         z_copy(target, 1).wait_send()
+
+    @pl.when(d > 0)
+    def _():
+        for p in range(chips):
+            next_copy(p).wait_send()
 
 
 def per_device(depth, count, amplitude, phase, kernel_phase, entry_field, cotangent):
@@ -367,7 +400,7 @@
             pltpu.VMEM(half_sum, F32),
             pltpu.VMEM(half_sum, F32),
             dma((8,)),
-            dma((above, 2)), dma((above, 2)),
+            dma((above, 2)), dma((above, 2)), dma((chips,)),
             dma((above, chips)), dma((above, chips)),
             dma((above, chips)), dma((above, chips)),
             dma((chips,)), dma((chips,)), dma((chips,)), dma((chips,)),

time: 34.6 us -> 34.4 us (level)
  no operation moved by 1% of the time
where the time goes in v7:
time: 34.4 us; the launch traced here: 34.3 us
  Pallas kernels  32.8 us (95%)
  local copies, waits for them, and re-layouts  1.47 us (4%)
    pallas_call x1, Pallas kernels, per_device(): pl.pallas_call(functools.partial(kernel, depth, count), out_shape=jax.Sha...  32.8 us
    unnamed x1, local copies, waits for them, and re-layouts  1.47 us

profile of v7, /device:TPU:0, one launch (start us, length us, event | category | flops | bytes accessed | tf_op | source)
XLA Modules:
  0.0 34.3 jit_solution(7229374401699124976)
XLA Ops:
  0.0 32.8 %shard_map.82 = f32[2,1,32,256]{3,2,1,0:T(8,128)} custom-call(f32[32,256]{1,0:T(8,128)} %bitcast.6, f32[32,256]{1,0:T(8,128)} %bitcast.7, f32[256,256]{1,0:T(8,128)} %kern_hbm.1, f32[2,4,2,32,256]{4,3,2,1,0:T(8,128)} %bitcast.4, f32[2,256,256]{2,1,0:T(8,128)} %bitcast.5, bf16[4,256,768]{2,1,0:T(8,128)(2,1)} %constant.6.clone.wide_hbm, ...), custom_call_target="tpu_custom_call" | custom-call | tf_op jit(solution)/shard_map/pallas_call | solution.py:379
  32.8 1.5 %copy.10 = f32[2,1,32,256]{3,2,1,0:T(8,128)} copy(f32[2,1,32,256]{3,2,1,0:T(8,128)} %shard_map.82) | data formatting | bytes 131072

commit v8 on v7

--- a/solution.py
+++ b/solution.py
@@ -77,7 +77,7 @@
     depth, count, amp_hbm, phase_hbm, kern_hbm, psi_hbm, cot_hbm, wide_hbm, tall_hbm, shuffle_hbm, out_ref,
     amp_ref, phase_ref, kern_ref, psi_ref, wide, tall, shuffle_ref,
     x_ref, h_ref, tmp_ref, own_ref, t_ref, end_ref, give_ref, got_ref, keep_ref, land_ref, loaded,
-    z_send, z_recv, n_send, g_send, g_recv, c_send, c_recv, twin_send, twin_recv, r_send, r_recv,
+    z_send, z_recv, n_send, f_send, g_send, g_recv, c_send, c_recv, twin_send, twin_recv, r_send, r_recv,
 ):
     length = kern_ref.shape[0]
     half = length // 2
@@ -123,6 +123,11 @@
         def _():
             greet(d + 1, owner(p))
 
+        if depth >= 3:
+            @pl.when(d == 0)
+            def _():
+                greet(depth - 1, owner(p))
+
     greet(*twin)
 
     loads[0].wait()
@@ -131,7 +136,9 @@
     own_ref[0] = amp_ref[...] * cos_t
     own_ref[1] = amp_ref[...] * sin_t
 
-    pl.semaphore_wait(barrier, d + (chips - 1) * jnp.minimum(d, 1) + chips)
+    lead = 1 - jnp.minimum(needed, 1)
+    peers = jnp.minimum(d, 1) + (lead if depth >= 3 else 0)
+    pl.semaphore_wait(barrier, d + (chips - 1) * peers + chips)
 
     def z_copy(target, c):
         return pltpu.make_async_remote_copy(
@@ -147,10 +154,22 @@
             device_id=(d - 1, owner(p)), device_id_type=MESH,
         )
 
+    def far_copy(p):
+        return pltpu.make_async_remote_copy(
+            src_ref=own_ref.at[1], dst_ref=t_ref.at[0, chip, core, 1],
+            send_sem=f_send.at[p], recv_sem=g_recv.at[0, chips - p],
+            device_id=(0, owner(p)), device_id_type=MESH,
+        )
+
     def z_start(target):
         @pl.when(target < d - 1)
         def _():
             z_copy(target, 0).start()
+            if depth >= 3:
+                @pl.when(jnp.logical_and(d == depth - 1, target == 0))
+                def _():
+                    for p in range(1, chips):
+                        far_copy(p).start()
             z_copy(target, 1).start()
 
         @pl.when(target == d - 1)
@@ -158,8 +177,6 @@
             for p in range(chips):
                 next_copy(p).start()
 
-    lead = 1 - jnp.minimum(needed, 1)
-
     def post(g):
         target = g + lead
 
@@ -169,11 +186,12 @@
 
     post(-1)
 
-    def g_copy(s, p, part=slice(None)):
+    def g_copy(s, p, part):
+        half_at = part.start
         block = t_ref.at[s, chip, core, part]
         return pltpu.make_async_remote_copy(
             src_ref=block, dst_ref=block,
-            send_sem=g_send.at[s, p], recv_sem=g_recv.at[s, chips - p],
+            send_sem=g_send.at[s, p, half_at], recv_sem=g_recv.at[s, chips - p],
             device_id=(d, owner(p)), device_id_type=MESH,
         )
 
@@ -191,8 +209,11 @@
             for c in (0, 1):
                 pltpu.make_async_copy(
                     own_ref.at[c], t_ref.at[s, chip, core, c], z_recv.at[s, c]).wait()
-                for p in range(1, chips):
-                    g_copy(s, p, pl.ds(c, 1)).start()
+
+                @pl.when(jnp.logical_or(c == 0, jnp.logical_or(s > 0, d > 0)))
+                def _():
+                    for p in range(1, chips):
+                        g_copy(s, p, pl.ds(c, 1)).start()
             c_copy(s, 0).start()
 
     def pass_on(s, p):
@@ -353,7 +374,11 @@
     @pl.loop(0, jnp.maximum(needed - 1, 0))
     def _(s):
         for p in range(1, chips):
-            g_copy(s, p).wait_send()
+            g_copy(s, p, pl.ds(0, 1)).wait_send()
+
+            @pl.when(jnp.logical_or(s > 0, d > 0))
+            def _():
+                g_copy(s, p, pl.ds(1, 1)).wait_send()
 
     @pl.loop(0, jnp.maximum(d - 1, 0))
     def _(target):
@@ -364,6 +389,12 @@
     def _():
         for p in range(chips):
             next_copy(p).wait_send()
+
+    if depth >= 3:
+        @pl.when(d == depth - 1)
+        def _():
+            for p in range(1, chips):
+                far_copy(p).wait_send()
 
 
 def per_device(depth, count, amplitude, phase, kernel_phase, entry_field, cotangent):
@@ -400,8 +431,8 @@
             pltpu.VMEM(half_sum, F32),
             pltpu.VMEM(half_sum, F32),
             dma((8,)),
-            dma((above, 2)), dma((above, 2)), dma((chips,)),
-            dma((above, chips)), dma((above, chips)),
+            dma((above, 2)), dma((above, 2)), dma((chips,)), dma((chips,)),
+            dma((above, chips, 2)), dma((above, chips)),
             dma((above, chips)), dma((above, chips)),
             dma((chips,)), dma((chips,)), dma((chips,)), dma((chips,)),
         ],

time: 34.4 us -> 34.6 us (level)
  no operation moved by 1% of the time
where the time goes in v8:
time: 34.6 us; the launch traced here: 34.4 us
  Pallas kernels  32.9 us (95%)
  local copies, waits for them, and re-layouts  1.47 us (4%)
    pallas_call x1, Pallas kernels, per_device(): pl.pallas_call(functools.partial(kernel, depth, count), out_shape=jax.Sha...  32.9 us
    unnamed x1, local copies, waits for them, and re-layouts  1.47 us

profile of v8, /device:TPU:0, one launch (start us, length us, event | category | flops | bytes accessed | tf_op | source)
XLA Modules:
  0.0 34.4 jit_solution(7555609386140978769)
XLA Ops:
  0.0 32.9 %shard_map.82 = f32[2,1,32,256]{3,2,1,0:T(8,128)} custom-call(f32[32,256]{1,0:T(8,128)} %bitcast.6, f32[32,256]{1,0:T(8,128)} %bitcast.7, f32[256,256]{1,0:T(8,128)} %kern_hbm.1, f32[2,4,2,32,256]{4,3,2,1,0:T(8,128)} %bitcast.4, f32[2,256,256]{2,1,0:T(8,128)} %bitcast.5, bf16[4,256,768]{2,1,0:T(8,128)(2,1)} %constant.6.clone.wide_hbm, ...), custom_call_target="tpu_custom_call" | custom-call | tf_op jit(solution)/shard_map/pallas_call | solution.py:410
  32.9 1.5 %copy.10 = f32[2,1,32,256]{3,2,1,0:T(8,128)} copy(f32[2,1,32,256]{3,2,1,0:T(8,128)} %shard_map.82) | data formatting | bytes 131072

commit v9 on v8

--- a/solution.py
+++ b/solution.py
@@ -35,9 +35,9 @@
     shuffle[perm, np.arange(length)] = 1.0
     wide, tall = [], []
     for high, low in map(halves, lefts):
-        wide.append(np.concatenate([high, high, low], axis=1))
+        wide.append(np.concatenate([high, low], axis=0))
     for high, low in map(halves, lefts):
-        tall.append(np.concatenate([high, high, low], axis=0))
+        tall.append(np.concatenate([high, low], axis=0))
     return np.stack(wide), np.stack(tall), shuffle.astype(ml_dtypes.bfloat16)
 
 
@@ -64,13 +64,17 @@
 
 
 def right(v, tab, at):
+    rows, length = v.shape
     high, low = split(v)
-    return dot(jnp.concatenate([high, low, high], axis=1), tab[at])
+    main = dot(jnp.concatenate([high, low], axis=0), tab[at, :length])
+    return main[:rows] + (main[rows:] + dot(high, tab[at, length:]))
 
 
 def left(v, tab, at):
+    length = v.shape[0]
     high, low = split(v)
-    return dot(tab[at], jnp.concatenate([high, low, high], axis=0))
+    main = dot(tab[at], high)
+    return main[:length] + (main[length:] + dot(tab[at, :length], low))
 
 
 def kernel(

time: 34.6 us -> 34.4 us (level)
  no operation moved by 1% of the time
where the time goes in v9:
time: 34.4 us; the launch traced here: 34.2 us
  Pallas kernels  32.8 us (95%)
  local copies, waits for them, and re-layouts  1.47 us (4%)
    pallas_call x1, Pallas kernels, per_device(): pl.pallas_call(functools.partial(kernel, depth, count), out_shape=jax.Sha...  32.8 us
    unnamed x1, local copies, waits for them, and re-layouts  1.47 us

profile of v9, /device:TPU:0, one launch (start us, length us, event | category | flops | bytes accessed | tf_op | source)
XLA Modules:
  0.0 34.2 jit_solution(8670421113718837728)
XLA Ops:
  0.0 32.8 %shard_map.82 = f32[2,1,32,256]{3,2,1,0:T(8,128)} custom-call(f32[32,256]{1,0:T(8,128)} %bitcast.6, f32[32,256]{1,0:T(8,128)} %bitcast.7, f32[256,256]{1,0:T(8,128)} %kern_hbm.1, f32[2,4,2,32,256]{4,3,2,1,0:T(8,128)} %bitcast.4, f32[2,256,256]{2,1,0:T(8,128)} %bitcast.5, bf16[4,512,256]{2,1,0:T(8,128)(2,1)} %constant.4.clone.wide_hbm.tall_hbm, ...), custom_call_target="tpu_custom_call" | custom-call | tf_op jit(solution)/shard_map/pallas_call | solution.py:414
  32.8 1.5 %copy.10 = f32[2,1,32,256]{3,2,1,0:T(8,128)} copy(f32[2,1,32,256]{3,2,1,0:T(8,128)} %shard_map.82) | data formatting | bytes 131072

commit v10 on v8

--- a/solution.py
+++ b/solution.py
@@ -223,10 +223,9 @@
             c_copy(s, p).start()
 
     def pass_all(s):
+        spread(s + 1)
         for p in [*range(1, chips), 0]:
             pass_on(s, p)
-            if p == min(1, chips - 1):
-                spread(s + 1)
 
     def arrived(s):
         for p in range(chips):

time: 34.6 us -> 34.6 us (level)
  no operation moved by 1% of the time
where the time goes in v10:
time: 34.6 us; the launch traced here: 34.4 us
  Pallas kernels  32.9 us (95%)
  local copies, waits for them, and re-layouts  1.47 us (4%)
    pallas_call x1, Pallas kernels, per_device(): pl.pallas_call(functools.partial(kernel, depth, count), out_shape=jax.Sha...  32.9 us
    unnamed x1, local copies, waits for them, and re-layouts  1.47 us

profile of v10, /device:TPU:0, one launch (start us, length us, event | category | flops | bytes accessed | tf_op | source)
XLA Modules:
  0.0 34.4 jit_solution(1714124503478988156)
XLA Ops:
  0.0 32.9 %shard_map.82 = f32[2,1,32,256]{3,2,1,0:T(8,128)} custom-call(f32[32,256]{1,0:T(8,128)} %bitcast.6, f32[32,256]{1,0:T(8,128)} %bitcast.7, f32[256,256]{1,0:T(8,128)} %kern_hbm.1, f32[2,4,2,32,256]{4,3,2,1,0:T(8,128)} %bitcast.4, f32[2,256,256]{2,1,0:T(8,128)} %bitcast.5, bf16[4,256,768]{2,1,0:T(8,128)(2,1)} %constant.6.clone.wide_hbm, ...), custom_call_target="tpu_custom_call" | custom-call | tf_op jit(solution)/shard_map/pallas_call | solution.py:409
  33.0 1.5 %copy.10 = f32[2,1,32,256]{3,2,1,0:T(8,128)} copy(f32[2,1,32,256]{3,2,1,0:T(8,128)} %shard_map.82) | data formatting | bytes 131072
